TPU v7x, 32 devices: a whole 2x2x4 slice. The times are simulated.
32 devices in a mesh: dp: 4 (over z), tm: 4 (over y, core), height: 2 (over x).
Axes of the slice: x: 2, y: 2, z: 4, core: 2. Of those that a mesh axis runs over, the one named last changes fastest.
Arguments:
- clip_inputs: bfloat16 [4, 8, 4, 16, 512], P('dp', 'tm', 'height'), may hold values from -6 to 6
- conv_in_weight: bfloat16 [13824, 512], P(('tm', 'height'), 'dp'), may hold values from -0.0546875 to 0.0546875
- group_gain: bfloat16 [512], P('dp'), may hold values from 0.099609375 to 1.8984375
- group_bias: bfloat16 [512], P('dp'), may hold values from -3 to 3
- conv_out_weight: bfloat16 [27, 512, 16], P(None, 'dp'), may hold values from -0.109375 to 0.109375
- out_bias: float32 [16], replicated, may hold values from -3 to 3
- patch_weight: bfloat16 [64, 3072], replicated, may hold values from -1.5 to 1.5
- patch_bias: bfloat16 [3072], replicated, may hold values from -3 to 3
- qkv_weight: bfloat16 [3072, 3072], P(('tm', 'height'), 'dp'), may hold values from -0.109375 to 0.109375
- qkv_bias: bfloat16 [3072], P('dp'), may hold values from -3 to 3
- q_gain: bfloat16 [128], replicated, may hold values from 0.099609375 to 1.8984375
- k_gain: bfloat16 [128], replicated, may hold values from 0.099609375 to 1.8984375
- frame_pos: int32 [8], P('tm'), may hold values from 0 to 63
- row_pos: int32 [2], P('height'), may hold values from 0 to 127
Outputs:
- latents: float32 [4, 8, 4, 256], P('dp', 'tm', 'height')
- queries: bfloat16 [4, 8, 2, 8, 1024], P(None, 'tm', 'height', None, 'dp')
- keys: bfloat16 [4, 8, 2, 8, 1024], P(None, 'tm', 'height', None, 'dp')
- values: bfloat16 [4, 8, 2, 8, 1024], P(None, 'tm', 'height', None, 'dp')
All inputs are finite; a program needn't handle non-finite values.
Results may differ from a plain program's by a relative error of at most 0.01.
Values may be sent and summed in bfloat16 or wider, within the bound.
No kernel may reach another device: no remote copies, remote signals or barrier semaphores. Data moves between devices by JAX's collectives and lax.ppermute only.
A program may use at most 64 MiB of HBM per device.

v0:
```python
import functools

import jax
import jax.numpy as jnp
import numpy as np
from jax import lax
from jax.experimental import pallas as pl
from jax.experimental.pallas import tpu as pltpu
from jax.sharding import PartitionSpec as P

HD = 128
GROUPS = 32
TAPS = 27


norm_eps = 1e-06
latent_scale = 0.476986
rope_base = 256.0
time_dims = 16
row_dims = 56


def from_behind(value, axis, steps):
    count = lax.axis_size(axis)
    first, last = (max(0, -steps), min(count, count - steps))
    return lax.ppermute(value, axis, [(source, source + steps) for source in range(first, last)])


def padded_2(block, sides, width):
    for axis, dim in sides:
        count = lax.axis_size(axis)
        forward = [(i, i + 1) for i in range(count - 1)]
        backward = [(target, source) for source, target in forward]
        low = lax.ppermute(
            lax.slice_in_dim(block, block.shape[dim] - width, None, axis=dim), axis, forward
        )
        high = lax.ppermute(lax.slice_in_dim(block, 0, width, axis=dim), axis, backward)
        block = jnp.concatenate([low, block, high], axis=dim)
    return block


def repeat_first(block):
    return jnp.concatenate([block[:, :1], block[:, :1]], axis=1)


def time_join(block, earlier):
    start = jnp.where(lax.axis_index("tm") == 0, repeat_first(block), earlier)
    return jnp.concatenate([start, block], axis=1)


def rows_finish(grown):
    place = lax.axis_index("height")
    top = jnp.where(place == 0, grown[:, :, 1:2], grown[:, :, :1])
    bottom = jnp.where(place == lax.axis_size("height") - 1, grown[:, :, -2:-1], grown[:, :, -1:])
    inner = jnp.concatenate([top, grown[:, :, 1:-1], bottom], axis=2)
    return jnp.pad(inner, ((0, 0), (0, 0), (0, 0), (1, 1), (0, 0)), mode="edge")


def edges_before(block):
    earlier = from_behind(block, "tm", 1)
    longer = time_join(block, earlier)
    return rows_finish(padded_2(longer, (("height", 2),), 1))


def edges_norm(block):
    earlier = from_behind(block, "tm", 1)
    longer = time_join(block, earlier)
    return rows_finish(padded_2(longer, (("height", 2),), 1))


def convolve(padded, weight):
    clips = padded.shape[0]
    frames = padded.shape[1] - 2
    rows = padded.shape[2] - 2
    cols = padded.shape[3] - 2
    total = jnp.zeros((clips * frames * rows * cols, weight.shape[2]), jnp.float32)
    for shift_t in range(3):
        for shift_r in range(3):
            for shift_c in range(3):
                window = padded[
                    :,
                    shift_t : shift_t + frames,
                    shift_r : shift_r + rows,
                    shift_c : shift_c + cols,
                ]
                window = window.reshape(-1, padded.shape[4])
                total = total + jnp.dot(
                    window,
                    weight[9 * shift_t + 3 * shift_r + shift_c],
                    preferred_element_type=jnp.float32,
                )
    return total.reshape(clips, frames, rows, cols, weight.shape[2])


def section_freqs(dims):
    return jnp.power(rope_base, -jnp.arange(0, dims, 2, dtype=jnp.float32) / dims)


def rope_angles(tpos, hpos, width):
    frames = tpos.shape[0]
    rows = hpos.shape[0]
    cols = jnp.arange(width, dtype=jnp.float32)
    part_t = tpos[:, None, None, None] * section_freqs(time_dims)
    part_h = hpos[None, :, None, None] * section_freqs(row_dims)
    part_w = cols[None, None, :, None] * section_freqs(row_dims)
    shape = (frames, rows, width)
    return jnp.concatenate(
        [
            jnp.broadcast_to(part_t, shape + (time_dims // 2,)),
            jnp.broadcast_to(part_h, shape + (row_dims // 2,)),
            jnp.broadcast_to(part_w, shape + (row_dims // 2,)),
        ],
        axis=-1,
    )


def rotate(vectors, angles):
    pairs = vectors.reshape(vectors.shape[:-1] + (vectors.shape[-1] // 2, 2))
    first = pairs[..., 0]
    second = pairs[..., 1]
    cosine = jnp.cos(angles)[..., None, :]
    sine = jnp.sin(angles)[..., None, :]
    turned = jnp.stack([first * cosine - second * sine, first * sine + second * cosine], axis=-1)
    return turned.reshape(vectors.shape)


def rms_scale(vectors, gain):
    return (
        vectors
        * lax.rsqrt(jnp.mean(vectors * vectors, axis=-1, keepdims=True) + norm_eps)
        * gain.astype(jnp.float32)
    )


def shards(
    clip_inputs,
    conv_in_weight,
    group_gain,
    group_bias,
    conv_out_weight,
    out_bias,
    patch_weight,
    patch_bias,
    qkv_weight,
    qkv_bias,
    q_gain,
    k_gain,
    frame_pos,
    row_pos,
):
    channels = clip_inputs.shape[4]
    frames = clip_inputs.shape[1]
    rows = clip_inputs.shape[2]
    cols = clip_inputs.shape[3]
    padded = lax.all_gather(edges_before(clip_inputs), "dp", axis=0, tiled=True)
    clips = padded.shape[0]
    weight_in = lax.all_gather(conv_in_weight, ("tm", "height"), axis=0, tiled=True).reshape(
        TAPS, channels, -1
    )
    hidden = convolve(padded, weight_in)
    block_width = hidden.shape[4]
    group_width = channels // GROUPS
    local_groups = block_width // group_width
    grouped = hidden.reshape(clips, -1, local_groups, group_width)
    sums_local = jnp.sum(grouped, axis=(1, 3))
    squares_local = jnp.sum(grouped * grouped, axis=(1, 3))
    sums_all, squares_all = lax.psum((sums_local, squares_local), ("tm", "height"))
    count = float(
        frames * lax.axis_size("tm") * rows * lax.axis_size("height") * cols * group_width
    )
    mean = sums_all / count
    var = squares_all / count - mean * mean
    scaled = (grouped - mean[:, None, :, None]) * lax.rsqrt(var + norm_eps)[:, None, :, None]
    scaled = scaled.reshape(hidden.shape) * group_gain.astype(jnp.float32) + group_bias.astype(
        jnp.float32
    )
    normed = jax.nn.silu(scaled).astype(jnp.bfloat16)
    partial_latent = convolve(edges_norm(normed), conv_out_weight)
    own_sum = lax.psum_scatter(partial_latent, "dp", scatter_dimension=0, tiled=True)
    own_latent = (own_sum + out_bias) * latent_scale
    every_latent = lax.all_gather(own_latent.astype(jnp.bfloat16), "dp", axis=0, tiled=True)
    latent_dims = every_latent.shape[4]
    latents = own_latent.reshape(1, frames, rows, cols * latent_dims)
    tok_rows = rows // 2
    tok_cols = cols // 2
    patches = every_latent.reshape(clips, frames, tok_rows, 2, tok_cols, 2, latent_dims)
    patches = patches.transpose(0, 1, 2, 4, 3, 5, 6).reshape(-1, 4 * latent_dims)
    embedded = (
        jnp.dot(patches, patch_weight, preferred_element_type=jnp.float32)
        + patch_bias.astype(jnp.float32)
    ).astype(jnp.bfloat16)
    projected = jnp.dot(
        embedded,
        lax.all_gather(qkv_weight, ("tm", "height"), axis=0, tiled=True),
        preferred_element_type=jnp.float32,
    )
    projected = projected + qkv_bias.astype(jnp.float32)
    local_heads = qkv_weight.shape[1] // (3 * HD)
    projected = projected.reshape(clips, frames, tok_rows, tok_cols, local_heads, 3, HD)
    angles = rope_angles(frame_pos.astype(jnp.float32), row_pos.astype(jnp.float32), tok_cols)
    query = rotate(rms_scale(projected[..., 0, :], q_gain), angles)
    key = rotate(rms_scale(projected[..., 1, :], k_gain), angles)
    value = projected[..., 2, :]
    merged = (clips, frames, tok_rows, tok_cols, local_heads * HD)
    return (
        latents,
        query.reshape(merged).astype(jnp.bfloat16),
        key.reshape(merged).astype(jnp.bfloat16),
        value.reshape(merged).astype(jnp.bfloat16),
    )


LANES = 128
TILE = 16
GROUP = 16


def one_group_each(mesh, clip_inputs, conv_in_weight, conv_out_weight, qkv_weight):
    plane = mesh.shape["tm"] * mesh.shape["height"]
    return (
        clip_inputs.shape[:4] == (1, 2, 2, 16)
        and mesh.shape["height"] == 2
        and mesh.shape["tm"] == 4
        and mesh.shape["dp"] == 4
        and conv_in_weight.shape[1] == plane * GROUP
        and clip_inputs.shape[4] == GROUP * GROUPS
        and conv_out_weight.shape[2] == TILE
        and qkv_weight.shape[1] == 6 * HD
    )


def lane_shifts(lane):
    col = lane % 16
    row = lane // 16 % 2
    half = lane // 64

    def cols(left, mid, right):
        left = jnp.where(col == 0, left, pltpu.roll(left, 1, 1))
        right = jnp.where(col == 15, right, pltpu.roll(right, LANES - 1, 1))
        return mid + left + right

    def rows(up, mid, down):
        up = jnp.where(
            row == 1, pltpu.roll(up, 16, 1), jnp.where(half == 1, pltpu.roll(up, 48, 1), up)
        )
        down = jnp.where(
            row == 0,
            pltpu.roll(down, LANES - 16, 1),
            jnp.where(half == 0, pltpu.roll(down, LANES - 48, 1), down),
        )
        return mid + up + down

    return cols, rows


def tap_sums(y_ref, top, tiles):
    lane = lax.broadcasted_iota(jnp.int32, (TILE, LANES), 1)
    second = lane // 32 % 2 == 1
    cols, rows = lane_shifts(lane)
    sums = []
    before = None
    for tile in range(tiles):

        def part(tap):
            at = top + tap * TILE
            return y_ref[at : at + TILE, tile * LANES : (tile + 1) * LANES]

        oldest, older, now = (
            rows(*(cols(*(part(9 * i + 3 * j + l) for l in range(3))) for j in range(3)))
            for i in range(3)
        )
        turned = pltpu.roll(older, 32, 1)
        if before is None:
            start = jnp.where(second, pltpu.roll(oldest, 32, 1), oldest)
            total = now + jnp.where(second, turned, older) + start
        else:
            total = now + jnp.where(second, turned, pltpu.roll(before[1], 96, 1)) + before[0]
        before = (oldest, older)
        sums.append(total)
    return sums


def pack_kernel(
    w_hbm, qkv_hbm, patch_hbm, patch_bias_hbm, out_hbm, lines_ref,
    w_ref, qkv_ref, patch_ref, patch_bias_ref, rows_ref, out_ref, sems,
):
    plane, channels, width = out_ref.shape
    depth = w_ref.shape[0]
    rows = qkv_ref.shape[0]
    place = lax.axis_index("tm") * lax.axis_size("height") + lax.axis_index("height")
    at = pl.ds(pl.multiple_of(place * rows, LANES), rows)
    loads = [
        pltpu.make_async_copy(w_hbm, w_ref, sems.at[0]),
        pltpu.make_async_copy(qkv_hbm, qkv_ref, sems.at[1]),
        pltpu.make_async_copy(patch_hbm.at[:, at], patch_ref, sems.at[2]),
        pltpu.make_async_copy(patch_bias_hbm, patch_bias_ref, sems.at[3]),
    ]
    for load in loads:
        load.start()
    whole = depth // LANES * LANES
    loads[0].wait()
    turned = w_ref[...].T
    for to in range(plane):
        first = to // 2 * channels
        out_ref[to, :, :whole] = turned[first : first + channels, :whole]
    body = slice(0, whole)
    tail = slice(whole, width)
    stores = [
        pltpu.make_async_copy(out_ref.at[:, :, part], out_hbm.at[:, :, part], sems.at[4 + index])
        for index, part in enumerate((body, tail))
    ]
    stores[0].start()
    for load in loads[1:]:
        load.wait()
    merged = jnp.dot(patch_ref[...], qkv_ref[...], preferred_element_type=jnp.float32)
    lane = lax.broadcasted_iota(jnp.int32, (8, LANES), 1)
    for to in range(plane):
        first = to // 2 * channels
        mine = [merged[8 * to : 8 * to + 8, q * LANES : (q + 1) * LANES] for q in range(6)]
        upper = [pltpu.roll(mine[4], 64, 1), mine[4], pltpu.roll(mine[5], 64, 1), mine[5]]
        upper = jnp.concatenate(upper, axis=0)[:, 64:].astype(jnp.bfloat16)
        lower = turned[first : first + channels, whole:]
        out_ref[to, :, whole : whole + LANES] = jnp.concatenate([lower, upper], axis=1)
        out_ref[to, :, whole + LANES :] = jnp.concatenate(mine[:4], axis=0).astype(jnp.bfloat16)
    stores[1].start()
    rows_ref[...] = patch_bias_ref[...].astype(jnp.float32).reshape(rows_ref.shape)
    count = rows // LANES
    bias = [rows_ref[pl.ds(count * place + part, 1), :] for part in range(count)]
    bias = jnp.broadcast_to(jnp.concatenate(bias, axis=1), (8, rows)).astype(jnp.bfloat16)
    bias = jnp.dot(bias, qkv_ref[...], preferred_element_type=jnp.float32)
    line = lax.broadcasted_iota(jnp.int32, (8, LANES), 0)
    lines = jnp.zeros((8, LANES), jnp.float32)
    for part in range(bias.shape[1] // LANES):
        lines = jnp.where(line == part, bias[:, part * LANES : (part + 1) * LANES], lines)
    lines_ref[...] = lines
    for store in stores:
        store.wait()


def column(row_ref, first, size):
    length = row_ref.shape[0]
    row = row_ref[...].astype(jnp.float32).reshape(1, length)
    line = lax.broadcasted_iota(jnp.int32, (size, length), 0)
    lane = lax.broadcasted_iota(jnp.int32, (size, length), 1)
    picked = jnp.where(lane == line + first, jnp.broadcast_to(row, (size, length)), 0.0)
    return jnp.sum(picked, axis=1, keepdims=True)


def table_kernel(
    frame_ref, row_pos_ref, freq_ref, gain_hbm, bias_hbm, out_bias_hbm, qkv_hbm, q_hbm, k_hbm,
    scale_ref, table_ref,
    gain_v, bias_v, out_bias_v, qkv_v, q_v, k_v, sems,
):
    pairs = (
        (gain_hbm, gain_v), (bias_hbm, bias_v), (out_bias_hbm, out_bias_v),
        (qkv_hbm, qkv_v), (q_hbm, q_v), (k_hbm, k_v),
    )
    loads = [
        pltpu.make_async_copy(source, to, sems.at[index])
        for index, (source, to) in enumerate(pairs)
    ]
    for load in loads:
        load.start()
    shape = (TILE, LANES)
    line = lax.broadcasted_iota(jnp.int32, shape, 0)
    lane = lax.broadcasted_iota(jnp.int32, shape, 1)
    frame = jnp.where(line // 8 == 0, frame_ref[0], frame_ref[1]).astype(jnp.float32)
    row = jnp.broadcast_to(row_pos_ref[0], shape).astype(jnp.float32)
    spot = jnp.where(lane < 72, row, (line % 8).astype(jnp.float32))
    angles = jnp.where(lane < 16, frame, spot) * freq_ref[...]
    table_ref[:16] = jnp.cos(angles)
    sine = jnp.sin(angles)
    table_ref[16:32] = jnp.where(lane % 2 == 0, -sine, sine)
    for load in loads:
        load.wait()
    first = lax.axis_index("tm") // 2 * (4 * GROUP)
    scale_ref[:, 0:1] = column(gain_v, first, 4 * GROUP)
    scale_ref[:, 1:2] = column(bias_v, first, 4 * GROUP)
    table_ref[32:48] = jnp.broadcast_to(column(out_bias_v, 0, TILE), shape)
    table_ref[48:49] = q_v[...].astype(jnp.float32).reshape(1, HD)
    table_ref[49:50] = k_v[...].astype(jnp.float32).reshape(1, HD)
    table_ref[50:56] = qkv_v[...].astype(jnp.float32).reshape(6, LANES)


def arrange_kernel(*refs):
    pieces, (keep_ref, send_ref, all_ref) = refs[:4], refs[4:]
    side = lax.axis_index("height")
    layer = lax.axis_index("dp")
    for step, piece in enumerate(pieces):
        all_ref[(layer + 4 - step) % 4] = piece[...]
    for core in range(2):
        keep_ref[core] = all_ref[2 * side + core]
        send_ref[core] = all_ref[2 - 2 * side + core]


def join_kernel(w_ref, lines_ref, wt_ref):
    plane, width, lanes = w_ref.shape
    channels = wt_ref.shape[1]
    depth = TAPS * channels // plane
    for group in range(width // GROUP):
        for tap in range(TAPS):
            start = tap * channels
            end = start + channels
            at = (group * TAPS + tap) * GROUP
            while start < end:
                source = start // depth
                stop = min(end, (source + 1) * depth)
                wt_ref[
                    at : at + GROUP, start - tap * channels : stop - tap * channels
                ] = w_ref[
                    source,
                    group * GROUP : (group + 1) * GROUP,
                    start - source * depth : stop - source * depth,
                ]
                start = stop
    total = w_ref[0, :, lanes - 2 * LANES :].astype(jnp.float32)
    for source in range(1, plane):
        total = total + w_ref[source, :, lanes - 2 * LANES :].astype(jnp.float32)
    low = lax.broadcasted_iota(jnp.int32, (8, LANES), 1) < 64
    parts = [total[8 * q : 8 * q + 8, LANES:] for q in range(4)]
    for q in range(2):
        one = total[16 * q : 16 * q + 8, :LANES]
        two = total[16 * q + 8 : 16 * q + 16, :LANES]
        parts.append(jnp.where(low, pltpu.roll(one, 64, 1), two))
    parts += [lines_ref[...], jnp.zeros((8, LANES), jnp.float32)]
    share = jnp.concatenate(
        [jnp.concatenate(parts[:4], axis=1), jnp.concatenate(parts[4:], axis=1)], axis=0
    )
    wt_ref[width * TAPS :] = share.astype(jnp.bfloat16)


def place_clip(pieces, x_ref):
    place = lax.axis_index("tm") // 2 * 4 + lax.axis_index("height")
    for flip, piece in zip((0, 1, 4, 5), pieces):
        for core in range(2):
            x_ref[(place ^ flip) + 2 * core] = piece[core]


def normed_half(x_ref, wt_ref, y_ref, scale_ref, half):
    channels = x_ref.shape[2]
    tiles = x_ref.shape[0] // 2
    taps = TAPS * GROUP
    count = float(tiles * LANES * GROUP)
    y_ref[...] = lax.dot_general(
        wt_ref[: 2 * taps],
        x_ref[...].reshape(tiles * LANES, channels),
        (((1,), (1,)), ((), ())),
        preferred_element_type=jnp.float32,
    )
    normed = []
    for group in range(2):
        hidden = tap_sums(y_ref, group * taps, tiles)
        at = pl.ds(pl.multiple_of((2 * half + group) * GROUP, GROUP), GROUP)
        mean = jnp.sum(sum(hidden), keepdims=True) / count
        square = jnp.sum(sum(part * part for part in hidden), keepdims=True) / count
        scale = lax.rsqrt(square - mean * mean + norm_eps)
        parts = []
        for part in hidden:
            scaled = (part - mean) * scale * scale_ref[at, 0:1] + scale_ref[at, 1:2]
            parts.append((scaled / (1.0 + jnp.exp(-scaled))).astype(jnp.bfloat16))
        normed.append(jnp.concatenate(parts, axis=1))
    return jnp.concatenate(normed, axis=0)


def own_half_kernel(
    x0_ref, x1_ref, x2_ref, x3_ref, wt_ref, scale_ref, out_ref, x_ref, y_ref
):
    place_clip((x0_ref, x1_ref, x2_ref, x3_ref), x_ref)
    half = lax.axis_index("tm") % 2
    out_ref[...] = normed_half(x_ref, wt_ref, y_ref, scale_ref, half)


def conv_kernel(
    x_ref, normed_ref, wt_ref, scale_ref, w2_ref, out_ref, y_ref, n_ref
):
    tiles = x_ref.shape[0] // 2
    half = lax.axis_index("tm") % 2
    n_ref[pl.ds(pl.multiple_of(half * 2 * GROUP, 2 * GROUP), 2 * GROUP)] = normed_ref[...]
    other = normed_half(x_ref, wt_ref, y_ref, scale_ref, 1 - half)
    n_ref[pl.ds(pl.multiple_of((1 - half) * 2 * GROUP, 2 * GROUP), 2 * GROUP)] = other
    y_ref[: TAPS * TILE] = jnp.dot(w2_ref[...], n_ref[...], preferred_element_type=jnp.float32)
    low = lax.broadcasted_iota(jnp.int32, (8, LANES), 1) < 64
    layers = out_ref.shape[0] // (2 * tiles)
    for tile, part in enumerate(tap_sums(y_ref, 0, tiles)):
        turned = pltpu.roll(part, 64, 1)
        near = jnp.where(low, part[:8], turned[8:])
        far = jnp.where(low, turned[:8], part[8:])
        for layer in range(layers):
            out_ref[layer * 2 * tiles + 2 * tile] = near
            out_ref[layer * 2 * tiles + 2 * tile + 1] = far


def token_kernel(
    p_ref, m0_ref, m1_ref, m2_ref, m3_ref, table_ref,
    lat_ref, q_ref, k_ref, v_ref, m_ref,
):
    spot = lax.axis_index("tm") * 2 + lax.axis_index("height")
    lines = jnp.zeros((8, LANES), jnp.float32)
    for flip, ref in ((0, m0_ref), (1, m1_ref), (4, m2_ref), (5, m3_ref)):
        for core in range(2):
            share = ref[core].astype(jnp.float32)
            at = spot ^ flip ^ (2 * core)
            m_ref[at, :, : 4 * LANES] = share[:8]
            m_ref[at, :, 4 * LANES :] = share[8:, : 2 * LANES]
            lines = lines + share[8:, 2 * LANES : 3 * LANES]
    low = lax.broadcasted_iota(jnp.int32, (8, LANES), 1) < 64
    pairs = []
    for side in range(2):
        one, two = (
            sum(p_ref[4 * index + 2 * core + side] for index in range(p_ref.shape[0] // 4))
            for core in range(2)
        )
        top = jnp.where(low, one, pltpu.roll(two, 64, 1))
        bottom = jnp.where(low, pltpu.roll(one, 64, 1), two)
        pairs.append(jnp.concatenate([top, bottom], axis=0))
    total = jnp.concatenate(pairs, axis=1)
    lat = (total + table_ref[32:48, :1]) * latent_scale
    clips = lat.shape[1] // 64
    tokens = clips * 16
    place = lax.axis_index("dp")
    own = lat[:, :LANES]
    for pair in range(1, clips // 2):
        own = jnp.where(place // 2 == pair, lat[:, pair * LANES : (pair + 1) * LANES], own)
    own = jnp.where(place % 2 == 1, pltpu.roll(own, 64, 1), own)
    turned = own.T[:64]
    wide = jnp.concatenate([turned] * 16, axis=1)
    spot = lax.broadcasted_iota(jnp.int32, wide.shape, 0) % 16
    spread = lax.broadcasted_iota(jnp.int32, wide.shape, 1) // 16
    merged = jnp.sum(jnp.where(spot == spread, wide, 0.0).reshape(4, 16, 256), axis=1)
    lat_ref[0, 0] = merged[:2]
    lat_ref[0, 1] = merged[2:]

    lat_bf = lat.astype(jnp.bfloat16)
    token = lax.broadcasted_iota(jnp.int32, (tokens, clips * 64), 0)
    lane = lax.broadcasted_iota(jnp.int32, (tokens, clips * 64), 1)
    first = token // 8 * 32 + token % 8 * 2
    heads = q_ref.shape[2] // HD
    lines = lines[: 3 * heads] + table_ref[50:56]
    projected = jnp.concatenate([lines[part : part + 1] for part in range(3 * heads)], axis=1)
    merged = m_ref[...].reshape(64, 3 * HD * heads).astype(jnp.bfloat16)
    for a in range(2):
        for e in range(2):
            chosen = jnp.where(lane == first + (16 * a + e), 1.0, 0.0).astype(jnp.bfloat16)
            patch = lax.dot_general(
                chosen, lat_bf, (((1,), (1,)), ((), ())), preferred_element_type=jnp.float32
            ).astype(jnp.bfloat16)
            weight = merged[(2 * a + e) * TILE : (2 * a + e + 1) * TILE]
            projected = projected + jnp.dot(patch, weight, preferred_element_type=jnp.float32)

    even = lax.broadcasted_iota(jnp.int32, (tokens, HD), 1) % 2 == 0
    cosine = jnp.concatenate([table_ref[:16]] * clips, axis=0)
    sine = jnp.concatenate([table_ref[16:32]] * clips, axis=0)

    def turn(vectors, gain):
        square = jnp.mean(vectors * vectors, axis=-1, keepdims=True)
        vectors = vectors * lax.rsqrt(square + norm_eps) * gain
        swapped = jnp.where(even, pltpu.roll(vectors, HD - 1, 1), pltpu.roll(vectors, 1, 1))
        return vectors * cosine + swapped * sine

    def keep(ref, head, value):
        value = value.reshape(tokens // 8, 8, HD).astype(jnp.bfloat16)
        ref[:, :, head * HD : (head + 1) * HD] = value

    for head in range(heads):
        at = 3 * HD * head
        keep(q_ref, head, turn(projected[:, at : at + HD], table_ref[48:49]))
        keep(k_ref, head, turn(projected[:, at + HD : at + 2 * HD], table_ref[49:50]))
        keep(v_ref, head, projected[:, at + 2 * HD : at + 3 * HD])


def rope_freqs():
    freqs = []
    for dims in (time_dims, row_dims, row_dims):
        freqs.append(rope_base ** (-np.arange(0, dims, 2, dtype=np.float64) / dims))
    return np.repeat(np.concatenate(freqs), 2)[None].astype(np.float32)


def vmem(count):
    return [pl.BlockSpec(memory_space=pltpu.VMEM)] * count


def grouped(
    clip_inputs,
    conv_in_weight,
    group_gain,
    group_bias,
    conv_out_weight,
    out_bias,
    patch_weight,
    patch_bias,
    qkv_weight,
    qkv_bias,
    q_gain,
    k_gain,
    frame_pos,
    row_pos,
):
    plane_axes = ("tm", "height")
    clips = lax.axis_size("dp")
    steps = lax.axis_size("tm")
    plane = steps * lax.axis_size("height")
    channels = clip_inputs.shape[4]
    depth = conv_in_weight.shape[0]

    width = -(-depth // LANES) * LANES + LANES
    hbm = pl.BlockSpec(memory_space=pltpu.HBM)
    wide = pltpu.CompilerParams(vmem_limit_bytes=60 * 1024 * 1024)
    limit = pltpu.CompilerParams(vmem_limit_bytes=32 * 1024 * 1024)
    small = pl.CostEstimate(flops=10**6, bytes_accessed=10**6, transcendentals=0)
    with jax.named_scope("weight_by_group"):
        packed, lines = pl.pallas_call(
            pack_kernel,
            out_shape=(
                jax.ShapeDtypeStruct((plane, 2 * GROUP, width), jnp.bfloat16),
                jax.ShapeDtypeStruct((8, LANES), jnp.float32),
            ),
            in_specs=[hbm] * 4,
            out_specs=(hbm, vmem(1)[0]),
            scratch_shapes=[
                pltpu.VMEM(conv_in_weight.shape, jnp.bfloat16),
                pltpu.VMEM(qkv_weight.shape, jnp.bfloat16),
                pltpu.VMEM((patch_weight.shape[0], qkv_weight.shape[0]), jnp.bfloat16),
                pltpu.VMEM(patch_bias.shape, jnp.bfloat16),
                pltpu.VMEM((patch_bias.shape[0] // LANES, LANES), jnp.float32),
                pltpu.VMEM((plane, 2 * GROUP, width), jnp.bfloat16),
                pltpu.SemaphoreType.DMA((6,)),
            ],
            compiler_params=wide,
            cost_estimate=pl.CostEstimate(flops=10**8, bytes_accessed=10**6, transcendentals=0),
            name="pack_weights",
        )(conv_in_weight, qkv_weight, patch_weight, patch_bias)
        weight = lax.all_to_all(packed, plane_axes, 0, 0, tiled=True)
    with jax.named_scope("gather_clips"):
        own = clip_inputs.reshape(64, channels)
        layers = []
        for step in range(clips):
            pairs = []
            for layer in range(clips):
                for tm in range(steps):
                    to = (layer // 2 * 2 + tm % 2 + step) % clips
                    pairs.append((layer * steps + tm, to * steps + tm // 2 * 2 + layer % 2))
            layers.append(lax.ppermute(own, ("dp", "tm"), pairs))
    with jax.named_scope("spread_clips"):
        keep, send = pl.pallas_call(
            arrange_kernel,
            out_shape=(jax.ShapeDtypeStruct((2, 64, channels), jnp.bfloat16),) * 2,
            in_specs=vmem(4),
            out_specs=tuple(vmem(2)),
            scratch_shapes=[pltpu.VMEM((4, 64, channels), jnp.bfloat16)],
            compiler_params=limit,
            cost_estimate=small,
            name="arrange_clips",
        )(*layers)
        pieces = [keep]
        for flip in (1, 4, 5):
            pairs = [(i, i ^ flip) for i in range(plane)]
            pieces.append(lax.ppermute(send if flip % 2 else keep, plane_axes, pairs))
    with jax.named_scope("small_weights"):
        first = lax.axis_index("tm") // 2 * (4 * GROUP)
        weight_out = lax.dynamic_slice_in_dim(conv_out_weight, first, 4 * GROUP, axis=1)
        weight_out = weight_out.transpose(0, 2, 1).reshape(TAPS * TILE, 4 * GROUP)
        smem = pl.BlockSpec(memory_space=pltpu.SMEM)
        small_arrays = (group_gain, group_bias, out_bias, qkv_bias, q_gain, k_gain)
        scale, table = pl.pallas_call(
            table_kernel,
            out_shape=(
                jax.ShapeDtypeStruct((4 * GROUP, 2), jnp.float32),
                jax.ShapeDtypeStruct((56, LANES), jnp.float32),
            ),
            in_specs=[smem, smem, vmem(1)[0]] + [hbm] * 6,
            out_specs=tuple(vmem(2)),
            scratch_shapes=[pltpu.VMEM(array.shape, array.dtype) for array in small_arrays]
            + [pltpu.SemaphoreType.DMA((6,))],
            compiler_params=wide,
            cost_estimate=small,
            name="tables",
        )(frame_pos, row_pos, rope_freqs(), *small_arrays)
    with jax.named_scope("join_weights"):
        joined = pl.pallas_call(
            join_kernel,
            out_shape=jax.ShapeDtypeStruct((2 * GROUP * TAPS + 16, channels), jnp.bfloat16),
            in_specs=vmem(2),
            out_specs=vmem(1)[0],
            compiler_params=limit,
            cost_estimate=small,
            name="join_weights",
        )(weight, lines)
        joined_pair = lax.ppermute(joined, "tm", [(i, i ^ 1) for i in range(steps)])
    with jax.named_scope("merged_projection"):
        share = jnp.stack([joined[-16:], joined_pair[-16:]])
        shares = [share]
        for flip in (1, 4, 5):
            pairs = [(i, i ^ flip) for i in range(plane)]
            shares.append(lax.ppermute(share, plane_axes, pairs))

    flops = 2 * clips * steps * LANES * TAPS * TILE * (channels + 16)
    cost = pl.CostEstimate(flops=flops // 2, bytes_accessed=10**6, transcendentals=0)
    product = pltpu.VMEM((2 * TAPS * GROUP, steps * LANES), jnp.float32)
    normed, clip = pl.pallas_call(
        own_half_kernel,
        out_shape=(
            jax.ShapeDtypeStruct((2 * GROUP, steps * LANES), jnp.bfloat16),
            jax.ShapeDtypeStruct((plane, 64, channels), jnp.bfloat16),
        ),
        in_specs=vmem(6),
        out_specs=tuple(vmem(2)),
        scratch_shapes=[product],
        compiler_params=limit,
        cost_estimate=pl.CostEstimate(flops=4 * 10**10, bytes_accessed=10**6, transcendentals=0),
        name="own_channels",
    )(*pieces, joined, scale)
    partial = pl.pallas_call(
        conv_kernel,
        out_shape=jax.ShapeDtypeStruct((clips * plane, 8, LANES), jnp.float32),
        in_specs=vmem(5),
        out_specs=vmem(1)[0],
        scratch_shapes=[product, pltpu.VMEM((4 * GROUP, steps * LANES), jnp.bfloat16)],
        compiler_params=limit,
        cost_estimate=cost,
        name="convolutions",
    )(clip, normed, joined_pair, scale, weight_out)

    with jax.named_scope("sum_latents"):
        partials = lax.all_to_all(partial, ("dp",) + plane_axes, 0, 0, tiled=True)

    heads = qkv_weight.shape[1] // (3 * HD)
    frames = clip_inputs.shape[1]
    tokens = jax.ShapeDtypeStruct((clips * frames, 8, heads * HD), jnp.bfloat16)
    latents, query, key, value = pl.pallas_call(
        token_kernel,
        out_shape=(jax.ShapeDtypeStruct((1, 2, 2, 256), jnp.float32), tokens, tokens, tokens),
        in_specs=vmem(6),
        out_specs=tuple(vmem(4)),
        scratch_shapes=[pltpu.VMEM((plane, 8, 6 * HD), jnp.float32)],
        compiler_params=limit,
        cost_estimate=pl.CostEstimate(flops=10**8, bytes_accessed=10**6, transcendentals=0),
        name="tokens",
    )(
        partials,
        *shares,
        table,
    )
    full = (clips, frames, 1, 8, heads * HD)
    return latents, query.reshape(full), key.reshape(full), value.reshape(full)


def pick(mesh, *arrays):
    if one_group_each(mesh, arrays[0], arrays[1], arrays[4], arrays[8]):
        return grouped(*arrays)
    return shards(*arrays)


def solution(mesh):
    placed = (
        P("dp", "tm", "height", None, None),
        P(("tm", "height"), "dp"),
        P("dp"),
        P("dp"),
        P(None, "dp", None),
        P(),
        P(),
        P(),
        P(("tm", "height"), "dp"),
        P("dp"),
        P(),
        P(),
        P("tm"),
        P("height"),
    )
    return jax.shard_map(
        functools.partial(pick, mesh),
        mesh=mesh,
        in_specs=placed,
        out_specs=(
            P("dp", "tm", "height", None),
            P(None, "tm", "height", None, "dp"),
            P(None, "tm", "height", None, "dp"),
            P(None, "tm", "height", None, "dp"),
        ),
        check_vma=False,
    )
```

profile of v0, /device:TPU:0, one launch (start us, length us, event | category | flops | bytes accessed | tf_op | source)
XLA Modules:
  0.0 48.4 jit_solution(14187768492454045656)
XLA Ops:
  0.6 0.0 copy-start
  0.6 2.9 %pack_weights.1 = (bf16[8,32,1920]{2,1,0:T(8,128)(2,1)}, f32[8,128]{1,0:T(8,128)}) custom-call(bf16[1728,128]{1,0:T(8,128)(2,1)} %w_hbm.1, bf16[384,768]{1,0:T(8,128)(2,1)} %qkv_hbm.2, bf16[64,3072]{1,0:T(8,128)(2,1)} %patch_hbm.1, bf16[3072]{0:T(1024)(128)(2,1)} %patch_bias_hbm.1), custom_call_target="tpu_custom_call" | custom-call | flops 100000000 | bytes 1000000 | tf_op jit(solution)/shard_map/weight_by_group/pack_weights/pallas_call | solution.py:611
  3.5 0.0 copy-start.4
  3.5 5.3 %all-to-all-start = ((bf16[8,32,1920]{2,1,0:T(8,128)(2,1)}), bf16[8,32,1920]{2,1,0:T(8,128)(2,1)S(1)}, u32[]{:S(2)}, u32[]{:S(2)}) async-start(bf16[8,32,1920]{2,1,0:T(8,128)(2,1)} %get-tuple-element.18), calls=%async_computation | async-start | bytes 1966080 | tf_op jit(solution)/shard_map/weight_by_group/all_to_all | solution.py:632
  8.9 0.7 %collective-permute-start = (bf16[64,512]{1,0:T(8,128)(2,1)S(1)}, bf16[64,512]{1,0:T(8,128)(2,1)S(1)}, u32[]{:S(2)}, u32[]{:S(2)}) collective-permute-start(bf16[64,512]{1,0:T(8,128)(2,1)S(1)} %bitcast.18), channel_id=1, source_target_pairs={{0,0},{2,8},{4,4},{6,12},{8,2},{10,10},{12,6},{14,14},{16,16},{18,... | collective-permute-start | bytes 196616 | tf_op jit(solution)/shard_map/gather_clips/ppermute | solution.py:642
  9.5 3.4 %collective-permute-start.1 = (bf16[64,512]{1,0:T(8,128)(2,1)S(1)}, bf16[64,512]{1,0:T(8,128)(2,1)S(1)}, u32[]{:S(2)}, u32[]{:S(2)}) collective-permute-start(bf16[64,512]{1,0:T(8,128)(2,1)S(1)} %bitcast.19), channel_id=1, source_target_pairs={{0,8},{2,16},{4,12},{6,20},{8,10},{10,18},{12,14},{14,22},{16,24},... | collective-permute-start | bytes 196616 | tf_op jit(solution)/shard_map/gather_clips/ppermute | solution.py:642
  13.0 2.6 %collective-permute-start.2 = (bf16[64,512]{1,0:T(8,128)(2,1)S(1)}, bf16[64,512]{1,0:T(8,128)(2,1)S(1)}, u32[]{:S(2)}, u32[]{:S(2)}) collective-permute-start(bf16[64,512]{1,0:T(8,128)(2,1)S(1)} %bitcast.20), channel_id=1, source_target_pairs={{0,16},{2,24},{4,20},{6,28},{8,18},{10,26},{12,22},{14,30},{16,0},... | collective-permute-start | bytes 196616 | tf_op jit(solution)/shard_map/gather_clips/ppermute | solution.py:642
  15.6 0.5 %collective-permute-start.3 = (bf16[64,512]{1,0:T(8,128)(2,1)S(1)}, bf16[64,512]{1,0:T(8,128)(2,1)S(1)}, u32[]{:S(2)}, u32[]{:S(2)}) collective-permute-start(bf16[64,512]{1,0:T(8,128)(2,1)S(1)} %bitcast.21), channel_id=1, source_target_pairs={{0,24},{2,0},{4,28},{6,4},{8,26},{10,2},{12,30},{14,6},{16,8},{18,... | collective-permute-start | bytes 196616 | tf_op jit(solution)/shard_map/gather_clips/ppermute | solution.py:642
  16.1 0.6 %collective-permute-done.1.refs_1_ = bf16[64,512]{1,0:T(8,128)(2,1)S(1)} collective-permute-done((bf16[64,512]{1,0:T(8,128)(2,1)S(1)}, bf16[64,512]{1,0:T(8,128)(2,1)S(1)}, u32[]{:S(2)}, u32[]{:S(2)}) %collective-permute-start.1) | collective-permute-done | bytes 65568 | tf_op jit(solution)/shard_map/gather_clips/ppermute | solution.py:642
  16.7 4.2 %collective-permute-done.2.refs_2_ = bf16[64,512]{1,0:T(8,128)(2,1)S(1)} collective-permute-done((bf16[64,512]{1,0:T(8,128)(2,1)S(1)}, bf16[64,512]{1,0:T(8,128)(2,1)S(1)}, u32[]{:S(2)}, u32[]{:S(2)}) %collective-permute-start.2) | collective-permute-done | bytes 65568 | tf_op jit(solution)/shard_map/gather_clips/ppermute | solution.py:642
  21.0 2.1 %collective-permute-start.4 = (bf16[2,64,512]{2,1,0:T(8,128)(2,1)S(1)}, bf16[2,64,512]{2,1,0:T(8,128)(2,1)S(1)}, u32[]{:S(2)}, u32[]{:S(2)}) collective-permute-start(bf16[2,64,512]{2,1,0:T(8,128)(2,1)S(1)} %get-tuple-element.17), channel_id=1, source_target_pairs={{0,1},{1,0},{2,3},{3,2},{4,5},{5,4},{6,7},{7,6},{8,9},{9,8},{10,11... | collective-permute-start | bytes 393224 | tf_op jit(solution)/shard_map/spread_clips/ppermute | solution.py:657
  23.0 1.5 %collective-permute-start.5 = (bf16[2,64,512]{2,1,0:T(8,128)(2,1)S(1)}, bf16[2,64,512]{2,1,0:T(8,128)(2,1)S(1)}, u32[]{:S(2)}, u32[]{:S(2)}) collective-permute-start(bf16[2,64,512]{2,1,0:T(8,128)(2,1)S(1)} %get-tuple-element.16.x0_ref), channel_id=1, source_target_pairs={{0,4},{1,5},{2,6},{3,7},{4,0},{5,1},{6,2},{7,3},{8,12},{9,13},{10,... | collective-permute-start | bytes 393224 | tf_op jit(solution)/shard_map/spread_clips/ppermute | solution.py:657
  24.5 0.1 collective-permute-start.6
  25.2 2.2 %tables.1 = (f32[64,2]{1,0:T(8,128)}, f32[56,128]{1,0:T(8,128)}) custom-call(s32[2]{0:T(128)} %frame_ref.1, s32[1]{0:T(128)S(6)} %copy.22.row_pos_ref, f32[1,128]{1,0:T(1,128)} %constant.27.clone.freq_ref, bf16[128]{0:T(256)(128)(2,1)} %gain_hbm.1, bf16[128]{0:T(256)(128)(2,1)} %bias_hbm.1, f32[16]{0:T(128)} %out_bias_hbm.1, bf16[768]{0:T(1024)(128)(2,1)} %qkv_hbm.3, ...), custom_call_target="tpu_custom_call" | custom-call | flops 1000000 | bytes 1000000 | tf_op jit(solution)/shard_map/small_weights/tables/pallas_call | solution.py:664
  27.4 0.0 copy-start.2
  27.4 0.1 constant_dynamic-slice_fusion
  27.5 0.6 %copy-done.2 = f32[8,128]{1,0:T(8,128)S(1)} copy-done((f32[8,128]{1,0:T(8,128)S(1)}, f32[8,128]{1,0:T(8,128)}, u32[]{:S(2)}) %copy-start.2) | copy-done | bytes 4120
  28.1 0.2 join_weights.1.wt_ref
  28.4 0.1 collective-permute-start.7
  28.4 0.5 %collective-permute-done.5.x2_ref = bf16[2,64,512]{2,1,0:T(8,128)(2,1)S(1)} collective-permute-done((bf16[2,64,512]{2,1,0:T(8,128)(2,1)S(1)}, bf16[2,64,512]{2,1,0:T(8,128)(2,1)S(1)}, u32[]{:S(2)}, u32[]{:S(2)}) %collective-permute-start.5) | collective-permute-done | bytes 131104 | tf_op jit(solution)/shard_map/spread_clips/ppermute | solution.py:657
  29.0 1.4 %collective-permute-done.6.x3_ref = bf16[2,64,512]{2,1,0:T(8,128)(2,1)S(1)} collective-permute-done((bf16[2,64,512]{2,1,0:T(8,128)(2,1)S(1)}, bf16[2,64,512]{2,1,0:T(8,128)(2,1)S(1)}, u32[]{:S(2)}, u32[]{:S(2)}) %collective-permute-start.6) | collective-permute-done | bytes 131104 | tf_op jit(solution)/shard_map/spread_clips/ppermute | solution.py:657
  30.4 1.2 %own_channels.1 = (bf16[32,512]{1,0:T(8,128)(2,1)S(1)}, bf16[8,64,512]{2,1,0:T(8,128)(2,1)S(1)}) custom-call(bf16[2,64,512]{2,1,0:T(8,128)(2,1)S(1)} %get-tuple-element.16.x0_ref, bf16[2,64,512]{2,1,0:T(8,128)(2,1)S(1)} %collective-permute-done.4.x1_ref, bf16[2,64,512]{2,1,0:T(8,128)(2,1)S(1)} %collective-permute-done.5.x2_ref, ...), custom_call_target="tpu_custom_call" | custom-call | flops 40000000000 | bytes 1000000 | tf_op jit(solution)/shard_map/own_channels/pallas_call | solution.py:699
  31.6 2.4 %convolutions.1 = f32[32,8,128]{2,1,0:T(8,128)} custom-call(bf16[8,64,512]{2,1,0:T(8,128)(2,1)S(1)} %get-tuple-element.21.x_ref, bf16[32,512]{1,0:T(8,128)(2,1)S(1)} %get-tuple-element.22.normed_ref, bf16[880,512]{1,0:T(8,128)(2,1)S(1)} %collective-permute-done.7.wt_ref, f32[64,2]{1,0:T(8,128)S(1)} %copy-done.1, bf16[432,64]{1,0:T(8,128)(2,1)S(1)} %bitcast.17), custom_call_target="tpu_custom_call" | custom-call | flops 467140608 | bytes 1000000 | tf_op jit(solution)/shard_map/convolutions/pallas_call | solution.py:712
  34.0 4.1 %all-to-all-start.1 = ((f32[32,8,128]{2,1,0:T(8,128)}), f32[32,8,128]{2,1,0:T(8,128)S(1)}, u32[]{:S(2)}, u32[]{:S(2)}) async-start(f32[32,8,128]{2,1,0:T(8,128)} %convolutions.1), calls=%async_computation.1 | async-start | bytes 262144 | tf_op jit(solution)/shard_map/sum_latents/all_to_all | solution.py:724
  38.1 2.7 %collective-permute-start.10 = (bf16[2,16,512]{2,1,0:T(8,128)(2,1)S(1)}, bf16[2,16,512]{2,1,0:T(8,128)(2,1)S(1)}, u32[]{:S(2)}, u32[]{:S(2)}) collective-permute-start(bf16[2,16,512]{2,1,0:T(8,128)(2,1)S(1)} %pad_maximum_fusion.m0_ref), channel_id=1, source_target_pairs={{0,5},{1,4},{2,7},{3,6},{4,1},{5,0},{6,3},{7,2},{8,13},{9,12},{10,... | collective-permute-start | bytes 98312 | tf_op jit(solution)/shard_map/merged_projection/ppermute | solution.py:694
  40.9 0.6 %collective-permute-start.8 = (bf16[2,16,512]{2,1,0:T(8,128)(2,1)S(1)}, bf16[2,16,512]{2,1,0:T(8,128)(2,1)S(1)}, u32[]{:S(2)}, u32[]{:S(2)}) collective-permute-start(bf16[2,16,512]{2,1,0:T(8,128)(2,1)S(1)} %pad_maximum_fusion.m0_ref), channel_id=1, source_target_pairs={{0,1},{1,0},{2,3},{3,2},{4,5},{5,4},{6,7},{7,6},{8,9},{9,8},{10,11... | collective-permute-start | bytes 98312 | tf_op jit(solution)/shard_map/merged_projection/ppermute | solution.py:694
  41.4 0.3 collective-permute-start.9
  41.7 1.5 %collective-permute-done.10.m3_ref = bf16[2,16,512]{2,1,0:T(8,128)(2,1)S(1)} collective-permute-done((bf16[2,16,512]{2,1,0:T(8,128)(2,1)S(1)}, bf16[2,16,512]{2,1,0:T(8,128)(2,1)S(1)}, u32[]{:S(2)}, u32[]{:S(2)}) %collective-permute-start.10) | collective-permute-done | bytes 32800 | tf_op jit(solution)/shard_map/merged_projection/ppermute | solution.py:694
  43.2 1.7 %collective-permute-done.8.m1_ref = bf16[2,16,512]{2,1,0:T(8,128)(2,1)S(1)} collective-permute-done((bf16[2,16,512]{2,1,0:T(8,128)(2,1)S(1)}, bf16[2,16,512]{2,1,0:T(8,128)(2,1)S(1)}, u32[]{:S(2)}, u32[]{:S(2)}) %collective-permute-start.8) | collective-permute-done | bytes 32800 | tf_op jit(solution)/shard_map/merged_projection/ppermute | solution.py:694
  44.9 0.4 collective-permute-done.9.m2_ref
  45.4 1.4 %all-to-all-done.1.p_ref = f32[32,8,128]{2,1,0:T(8,128)S(1)} async-done(((f32[32,8,128]{2,1,0:T(8,128)}), f32[32,8,128]{2,1,0:T(8,128)S(1)}, u32[]{:S(2)}, u32[]{:S(2)}) %all-to-all-start.1) | async-done | bytes 131104 | tf_op jit(solution)/shard_map/sum_latents/all_to_all | solution.py:724
  46.7 1.6 %tokens.1 = (f32[1,2,2,256]{3,2,1,0:T(2,128)}, bf16[8,8,256]{2,1,0:T(8,128)(2,1)}, bf16[8,8,256]{2,1,0:T(8,128)(2,1)}, bf16[8,8,256]{2,1,0:T(8,128)(2,1)}) custom-call(f32[32,8,128]{2,1,0:T(8,128)S(1)} %all-to-all-done.1.p_ref, bf16[2,16,512]{2,1,0:T(8,128)(2,1)S(1)} %pad_maximum_fusion.m0_ref, bf16[2,16,512]{2,1,0:T(8,128)(2,1)S(1)} %collective-permute-done.8.m1_ref, ...), custom_call_target="tpu_custom_call" | custom-call | flops 100000000 | bytes 1000000 | tf_op jit(solution)/shard_map/tokens/pallas_call | solution.py:729
  (15 shorter events, 0.1 us)
Async XLA Ops:
  0.6 26.8 %copy-start = (bf16[27,128,16]{1,2,0:T(8,128)(2,1)S(1)}, bf16[27,128,16]{1,2,0:T(8,128)(2,1)}, u32[]{:S(2)}) copy-start(bf16[27,128,16]{1,2,0:T(8,128)(2,1)} %param.19) | copy-start | bytes 331780
  3.5 5.3 %copy-start.4 = (bf16[1,2,2,16,512]{4,3,2,1,0:T(8,128)(2,1)S(1)}, bf16[1,2,2,16,512]{4,3,2,1,0:T(8,128)(2,1)}, u32[]{:S(2)}) copy-start(bf16[1,2,2,16,512]{4,3,2,1,0:T(8,128)(2,1)} %param.15) | copy-start | bytes 196612
  3.5 24.0 %all-to-all-start = ((bf16[8,32,1920]{2,1,0:T(8,128)(2,1)}), bf16[8,32,1920]{2,1,0:T(8,128)(2,1)S(1)}, u32[]{:S(2)}, u32[]{:S(2)}) async-start(bf16[8,32,1920]{2,1,0:T(8,128)(2,1)} %get-tuple-element.18), calls=%async_computation | async-start | bytes 1966080 | tf_op jit(solution)/shard_map/weight_by_group/all_to_all | solution.py:632
  8.9 7.2 %collective-permute-start = (bf16[64,512]{1,0:T(8,128)(2,1)S(1)}, bf16[64,512]{1,0:T(8,128)(2,1)S(1)}, u32[]{:S(2)}, u32[]{:S(2)}) collective-permute-start(bf16[64,512]{1,0:T(8,128)(2,1)S(1)} %bitcast.18), channel_id=1, source_target_pairs={{0,0},{2,8},{4,4},{6,12},{8,2},{10,10},{12,6},{14,14},{16,16},{18,... | collective-permute-start | bytes 196616 | tf_op jit(solution)/shard_map/gather_clips/ppermute | solution.py:642
  9.5 7.1 %collective-permute-start.1 = (bf16[64,512]{1,0:T(8,128)(2,1)S(1)}, bf16[64,512]{1,0:T(8,128)(2,1)S(1)}, u32[]{:S(2)}, u32[]{:S(2)}) collective-permute-start(bf16[64,512]{1,0:T(8,128)(2,1)S(1)} %bitcast.19), channel_id=1, source_target_pairs={{0,8},{2,16},{4,12},{6,20},{8,10},{10,18},{12,14},{14,22},{16,24},... | collective-permute-start | bytes 196616 | tf_op jit(solution)/shard_map/gather_clips/ppermute | solution.py:642
  13.0 7.9 %collective-permute-start.2 = (bf16[64,512]{1,0:T(8,128)(2,1)S(1)}, bf16[64,512]{1,0:T(8,128)(2,1)S(1)}, u32[]{:S(2)}, u32[]{:S(2)}) collective-permute-start(bf16[64,512]{1,0:T(8,128)(2,1)S(1)} %bitcast.20), channel_id=1, source_target_pairs={{0,16},{2,24},{4,20},{6,28},{8,18},{10,26},{12,22},{14,30},{16,0},... | collective-permute-start | bytes 196616 | tf_op jit(solution)/shard_map/gather_clips/ppermute | solution.py:642
  15.6 5.3 %collective-permute-start.3 = (bf16[64,512]{1,0:T(8,128)(2,1)S(1)}, bf16[64,512]{1,0:T(8,128)(2,1)S(1)}, u32[]{:S(2)}, u32[]{:S(2)}) collective-permute-start(bf16[64,512]{1,0:T(8,128)(2,1)S(1)} %bitcast.21), channel_id=1, source_target_pairs={{0,24},{2,0},{4,28},{6,4},{8,26},{10,2},{12,30},{14,6},{16,8},{18,... | collective-permute-start | bytes 196616 | tf_op jit(solution)/shard_map/gather_clips/ppermute | solution.py:642
  21.0 7.5 %collective-permute-start.4 = (bf16[2,64,512]{2,1,0:T(8,128)(2,1)S(1)}, bf16[2,64,512]{2,1,0:T(8,128)(2,1)S(1)}, u32[]{:S(2)}, u32[]{:S(2)}) collective-permute-start(bf16[2,64,512]{2,1,0:T(8,128)(2,1)S(1)} %get-tuple-element.17), channel_id=1, source_target_pairs={{0,1},{1,0},{2,3},{3,2},{4,5},{5,4},{6,7},{7,6},{8,9},{9,8},{10,11... | collective-permute-start | bytes 393224 | tf_op jit(solution)/shard_map/spread_clips/ppermute | solution.py:657
  23.0 5.9 %collective-permute-start.5 = (bf16[2,64,512]{2,1,0:T(8,128)(2,1)S(1)}, bf16[2,64,512]{2,1,0:T(8,128)(2,1)S(1)}, u32[]{:S(2)}, u32[]{:S(2)}) collective-permute-start(bf16[2,64,512]{2,1,0:T(8,128)(2,1)S(1)} %get-tuple-element.16.x0_ref), channel_id=1, source_target_pairs={{0,4},{1,5},{2,6},{3,7},{4,0},{5,1},{6,2},{7,3},{8,12},{9,13},{10,... | collective-permute-start | bytes 393224 | tf_op jit(solution)/shard_map/spread_clips/ppermute | solution.py:657
  24.5 5.9 %collective-permute-start.6 = (bf16[2,64,512]{2,1,0:T(8,128)(2,1)S(1)}, bf16[2,64,512]{2,1,0:T(8,128)(2,1)S(1)}, u32[]{:S(2)}, u32[]{:S(2)}) collective-permute-start(bf16[2,64,512]{2,1,0:T(8,128)(2,1)S(1)} %get-tuple-element.17), channel_id=1, source_target_pairs={{0,5},{1,4},{2,7},{3,6},{4,1},{5,0},{6,3},{7,2},{8,13},{9,12},{10,... | collective-permute-start | bytes 393224 | tf_op jit(solution)/shard_map/spread_clips/ppermute | solution.py:657
  27.4 0.7 %copy-start.2 = (f32[8,128]{1,0:T(8,128)S(1)}, f32[8,128]{1,0:T(8,128)}, u32[]{:S(2)}) copy-start(f32[8,128]{1,0:T(8,128)} %get-tuple-element.19.lines_ref) | copy-start | bytes 12292
  28.1 2.3 %copy-start.1 = (f32[64,2]{1,0:T(8,128)S(1)}, f32[64,2]{1,0:T(8,128)}, u32[]{:S(2)}) copy-start(f32[64,2]{1,0:T(8,128)} %get-tuple-element.20.scale_ref) | copy-start | bytes 1540
  28.4 3.3 %collective-permute-start.7 = (bf16[880,512]{1,0:T(8,128)(2,1)S(1)}, bf16[880,512]{1,0:T(8,128)(2,1)S(1)}, u32[]{:S(2)}, u32[]{:S(2)}) collective-permute-start(bf16[880,512]{1,0:T(8,128)(2,1)S(1)} %join_weights.1.wt_ref), channel_id=1, source_target_pairs={{0,2},{2,0},{4,6},{6,4},{1,3},{3,1},{5,7},{7,5},{8,10},{10,8},{12,... | collective-permute-start | bytes 2703368 | tf_op jit(solution)/shard_map/join_weights/ppermute | solution.py:688
  34.0 12.7 %all-to-all-start.1 = ((f32[32,8,128]{2,1,0:T(8,128)}), f32[32,8,128]{2,1,0:T(8,128)S(1)}, u32[]{:S(2)}, u32[]{:S(2)}) async-start(f32[32,8,128]{2,1,0:T(8,128)} %convolutions.1), calls=%async_computation.1 | async-start | bytes 262144 | tf_op jit(solution)/shard_map/sum_latents/all_to_all | solution.py:724
  38.1 8.6 %copy-start.3 = (f32[56,128]{1,0:T(8,128)S(1)}, f32[56,128]{1,0:T(8,128)}, u32[]{:S(2)}) copy-start(f32[56,128]{1,0:T(8,128)} %get-tuple-element.23.table_ref) | copy-start | bytes 86020
  38.1 5.1 %collective-permute-start.10 = (bf16[2,16,512]{2,1,0:T(8,128)(2,1)S(1)}, bf16[2,16,512]{2,1,0:T(8,128)(2,1)S(1)}, u32[]{:S(2)}, u32[]{:S(2)}) collective-permute-start(bf16[2,16,512]{2,1,0:T(8,128)(2,1)S(1)} %pad_maximum_fusion.m0_ref), channel_id=1, source_target_pairs={{0,5},{1,4},{2,7},{3,6},{4,1},{5,0},{6,3},{7,2},{8,13},{9,12},{10,... | collective-permute-start | bytes 98312 | tf_op jit(solution)/shard_map/merged_projection/ppermute | solution.py:694
  40.9 4.0 %collective-permute-start.8 = (bf16[2,16,512]{2,1,0:T(8,128)(2,1)S(1)}, bf16[2,16,512]{2,1,0:T(8,128)(2,1)S(1)}, u32[]{:S(2)}, u32[]{:S(2)}) collective-permute-start(bf16[2,16,512]{2,1,0:T(8,128)(2,1)S(1)} %pad_maximum_fusion.m0_ref), channel_id=1, source_target_pairs={{0,1},{1,0},{2,3},{3,2},{4,5},{5,4},{6,7},{7,6},{8,9},{9,8},{10,11... | collective-permute-start | bytes 98312 | tf_op jit(solution)/shard_map/merged_projection/ppermute | solution.py:694
  41.4 3.9 %collective-permute-start.9 = (bf16[2,16,512]{2,1,0:T(8,128)(2,1)S(1)}, bf16[2,16,512]{2,1,0:T(8,128)(2,1)S(1)}, u32[]{:S(2)}, u32[]{:S(2)}) collective-permute-start(bf16[2,16,512]{2,1,0:T(8,128)(2,1)S(1)} %pad_maximum_fusion.m0_ref), channel_id=1, source_target_pairs={{0,4},{1,5},{2,6},{3,7},{4,0},{5,1},{6,2},{7,3},{8,12},{9,13},{10,... | collective-permute-start | bytes 98312 | tf_op jit(solution)/shard_map/merged_projection/ppermute | solution.py:694
where the time goes:
time: 48.8 us; the launch traced here: 48.4 us
  starting transfers between devices  23.8 us (49%)
  waiting for transfers between devices  11.8 us (24%)
  Pallas kernels  10.6 us (22%)
  between operations  1.46 us (3%)
  local copies, waits for them, and re-layouts  0.7 us (1%)
    ppermute x4, starting transfers between devices, grouped(): layers.append(lax.ppermute(own, ('dp', 'tm'), pairs))  7.17 us
    all_to_all x1, starting transfers between devices, grouped(): weight = lax.all_to_all(packed, plane_axes, 0, 0, tiled=True)  5.31 us
    ppermute x4, waiting for transfers between devices, grouped(): layers.append(lax.ppermute(own, ('dp', 'tm'), pairs))  4.85 us
    all_to_all x1, starting transfers between devices, grouped(): partials = lax.all_to_all(partial, ('dp',) + plane_axes, 0, 0, tiled=True)  4.08 us
    ppermute x3, waiting for transfers between devices, grouped(): shares.append(lax.ppermute(share, plane_axes, pairs))  3.67 us
    ppermute x3, starting transfers between devices, grouped(): pieces.append(lax.ppermute(send if flip % 2 else keep, plane_axes, pairs))  3.61 us
    ppermute x3, starting transfers between devices, grouped(): shares.append(lax.ppermute(share, plane_axes, pairs))  3.55 us
    pallas_call x1, Pallas kernels, grouped(): pl.pallas_call(pack_kernel, out_shape=(jax.ShapeDtypeStruct((plane, 2 * G...  2.88 us
  transfers between devices with their start and end apart: 13, of which 8 were waited for; matrix products, arithmetic and copies ran while one was open for 0% of the time, Pallas kernels for 8%

commit v1 on v0

--- a/solution.py
+++ b/solution.py
@@ -383,7 +383,8 @@
 
 
 def arrange_kernel(*refs):
-    pieces, (keep_ref, send_ref, all_ref) = refs[:4], refs[4:]
+    pieces, (table_ref, keep_ref, send_ref, kept_table_ref, all_ref) = refs[:4], refs[4:]
+    kept_table_ref[...] = table_ref[...]
     side = lax.axis_index("height")
     layer = lax.axis_index("dp")
     for step, piece in enumerate(pieces):
@@ -471,7 +472,7 @@
 
 
 def conv_kernel(
-    x_ref, normed_ref, wt_ref, scale_ref, w2_ref, out_ref, y_ref, n_ref
+    x_ref, normed_ref, wt_ref, scale_ref, w2_ref, keep_ref, send_ref, y_ref, n_ref, out_ref
 ):
     tiles = x_ref.shape[0] // 2
     half = lax.axis_index("tm") % 2
@@ -479,19 +480,39 @@
     other = normed_half(x_ref, wt_ref, y_ref, scale_ref, 1 - half)
     n_ref[pl.ds(pl.multiple_of((1 - half) * 2 * GROUP, 2 * GROUP), 2 * GROUP)] = other
     y_ref[: TAPS * TILE] = jnp.dot(w2_ref[...], n_ref[...], preferred_element_type=jnp.float32)
+    high = lax.axis_index("tm") // 2
+    for tile, part in enumerate(tap_sums(y_ref, 0, tiles)):
+        out_ref[high ^ (tile // 2), tile % 2] = part
+    keep_ref[...] = out_ref[0]
+    send_ref[...] = out_ref[1]
+
+
+def spread_kernel(keep_ref, other_ref, *out_refs):
+    core = lax.axis_index("tm") % 2
+    side = lax.axis_index("height")
     low = lax.broadcasted_iota(jnp.int32, (8, LANES), 1) < 64
-    layers = out_ref.shape[0] // (2 * tiles)
-    for tile, part in enumerate(tap_sums(y_ref, 0, tiles)):
+    for flip, out_ref in enumerate(out_refs):
+        part = keep_ref[core ^ (flip // 2)] + other_ref[core ^ (flip // 2)]
         turned = pltpu.roll(part, 64, 1)
         near = jnp.where(low, part[:8], turned[8:])
         far = jnp.where(low, turned[:8], part[8:])
-        for layer in range(layers):
-            out_ref[layer * 2 * tiles + 2 * tile] = near
-            out_ref[layer * 2 * tiles + 2 * tile + 1] = far
+        out_ref[...] = jnp.where((side ^ (flip % 2)) == 0, near, far)
+
+
+def clips_kernel(p0_ref, p1_ref, p2_ref, p3_ref, out_ref, all_ref):
+    core = lax.axis_index("tm") % 2
+    side = lax.axis_index("height")
+    low = lax.broadcasted_iota(jnp.int32, (8, LANES), 1) < 64
+    for flip, ref in enumerate((p0_ref, p1_ref, p2_ref, p3_ref)):
+        all_ref[2 * (side ^ (flip % 2)) + (core ^ (flip // 2))] = ref[...]
+    for pair in range(2):
+        one, two = all_ref[2 * pair], all_ref[2 * pair + 1]
+        out_ref[pair, :8] = jnp.where(low, one, pltpu.roll(two, 64, 1))
+        out_ref[pair, 8:] = jnp.where(low, pltpu.roll(one, 64, 1), two)
 
 
 def token_kernel(
-    p_ref, m0_ref, m1_ref, m2_ref, m3_ref, table_ref,
+    p0_ref, p1_ref, p2_ref, p3_ref, m0_ref, m1_ref, m2_ref, m3_ref, table_ref,
     lat_ref, q_ref, k_ref, v_ref, m_ref,
 ):
     spot = lax.axis_index("tm") * 2 + lax.axis_index("height")
@@ -503,17 +524,8 @@
             m_ref[at, :, : 4 * LANES] = share[:8]
             m_ref[at, :, 4 * LANES :] = share[8:, : 2 * LANES]
             lines = lines + share[8:, 2 * LANES : 3 * LANES]
-    low = lax.broadcasted_iota(jnp.int32, (8, LANES), 1) < 64
-    pairs = []
-    for side in range(2):
-        one, two = (
-            sum(p_ref[4 * index + 2 * core + side] for index in range(p_ref.shape[0] // 4))
-            for core in range(2)
-        )
-        top = jnp.where(low, one, pltpu.roll(two, 64, 1))
-        bottom = jnp.where(low, pltpu.roll(one, 64, 1), two)
-        pairs.append(jnp.concatenate([top, bottom], axis=0))
-    total = jnp.concatenate(pairs, axis=1)
+    total = p0_ref[...] + p1_ref[...] + p2_ref[...] + p3_ref[...]
+    total = jnp.concatenate([total[0], total[1]], axis=1)
     lat = (total + table_ref[32:48, :1]) * latent_scale
     clips = lat.shape[1] // 64
     tokens = clips * 16
@@ -630,35 +642,7 @@
             name="pack_weights",
         )(conv_in_weight, qkv_weight, patch_weight, patch_bias)
         weight = lax.all_to_all(packed, plane_axes, 0, 0, tiled=True)
-    with jax.named_scope("gather_clips"):
-        own = clip_inputs.reshape(64, channels)
-        layers = []
-        for step in range(clips):
-            pairs = []
-            for layer in range(clips):
-                for tm in range(steps):
-                    to = (layer // 2 * 2 + tm % 2 + step) % clips
-                    pairs.append((layer * steps + tm, to * steps + tm // 2 * 2 + layer % 2))
-            layers.append(lax.ppermute(own, ("dp", "tm"), pairs))
-    with jax.named_scope("spread_clips"):
-        keep, send = pl.pallas_call(
-            arrange_kernel,
-            out_shape=(jax.ShapeDtypeStruct((2, 64, channels), jnp.bfloat16),) * 2,
-            in_specs=vmem(4),
-            out_specs=tuple(vmem(2)),
-            scratch_shapes=[pltpu.VMEM((4, 64, channels), jnp.bfloat16)],
-            compiler_params=limit,
-            cost_estimate=small,
-            name="arrange_clips",
-        )(*layers)
-        pieces = [keep]
-        for flip in (1, 4, 5):
-            pairs = [(i, i ^ flip) for i in range(plane)]
-            pieces.append(lax.ppermute(send if flip % 2 else keep, plane_axes, pairs))
-    with jax.named_scope("small_weights"):
-        first = lax.axis_index("tm") // 2 * (4 * GROUP)
-        weight_out = lax.dynamic_slice_in_dim(conv_out_weight, first, 4 * GROUP, axis=1)
-        weight_out = weight_out.transpose(0, 2, 1).reshape(TAPS * TILE, 4 * GROUP)
+    with jax.named_scope("tables"):
         smem = pl.BlockSpec(memory_space=pltpu.SMEM)
         small_arrays = (group_gain, group_bias, out_bias, qkv_bias, q_gain, k_gain)
         scale, table = pl.pallas_call(
@@ -675,6 +659,36 @@
             cost_estimate=small,
             name="tables",
         )(frame_pos, row_pos, rope_freqs(), *small_arrays)
+    with jax.named_scope("gather_clips"):
+        own = clip_inputs.reshape(64, channels)
+        layers = []
+        for step in range(clips):
+            pairs = []
+            for layer in range(clips):
+                for tm in range(steps):
+                    to = (layer // 2 * 2 + tm % 2 + step) % clips
+                    pairs.append((layer * steps + tm, to * steps + tm // 2 * 2 + layer % 2))
+            layers.append(lax.ppermute(own, ("dp", "tm"), pairs))
+    with jax.named_scope("spread_clips"):
+        keep, send, table = pl.pallas_call(
+            arrange_kernel,
+            out_shape=(jax.ShapeDtypeStruct((2, 64, channels), jnp.bfloat16),) * 2
+            + (jax.ShapeDtypeStruct(table.shape, table.dtype),),
+            in_specs=vmem(5),
+            out_specs=tuple(vmem(3)),
+            scratch_shapes=[pltpu.VMEM((4, 64, channels), jnp.bfloat16)],
+            compiler_params=limit,
+            cost_estimate=small,
+            name="arrange_clips",
+        )(*layers, table)
+        pieces = [keep]
+        for flip in (1, 4, 5):
+            pairs = [(i, i ^ flip) for i in range(plane)]
+            pieces.append(lax.ppermute(send if flip % 2 else keep, plane_axes, pairs))
+    with jax.named_scope("small_weights"):
+        first = lax.axis_index("tm") // 2 * (4 * GROUP)
+        weight_out = lax.dynamic_slice_in_dim(conv_out_weight, first, 4 * GROUP, axis=1)
+        weight_out = weight_out.transpose(0, 2, 1).reshape(TAPS * TILE, 4 * GROUP)
     with jax.named_scope("join_weights"):
         joined = pl.pallas_call(
             join_kernel,
@@ -709,19 +723,50 @@
         cost_estimate=pl.CostEstimate(flops=4 * 10**10, bytes_accessed=10**6, transcendentals=0),
         name="own_channels",
     )(*pieces, joined, scale)
-    partial = pl.pallas_call(
+    kept, sent = pl.pallas_call(
         conv_kernel,
-        out_shape=jax.ShapeDtypeStruct((clips * plane, 8, LANES), jnp.float32),
+        out_shape=(jax.ShapeDtypeStruct((2, TILE, LANES), jnp.float32),) * 2,
         in_specs=vmem(5),
-        out_specs=vmem(1)[0],
-        scratch_shapes=[product, pltpu.VMEM((4 * GROUP, steps * LANES), jnp.bfloat16)],
+        out_specs=tuple(vmem(2)),
+        scratch_shapes=[
+            product,
+            pltpu.VMEM((4 * GROUP, steps * LANES), jnp.bfloat16),
+            pltpu.VMEM((2, 2, TILE, LANES), jnp.float32),
+        ],
         compiler_params=limit,
         cost_estimate=cost,
         name="convolutions",
     )(clip, normed, joined_pair, scale, weight_out)
 
     with jax.named_scope("sum_latents"):
-        partials = lax.all_to_all(partial, ("dp",) + plane_axes, 0, 0, tiled=True)
+        other = lax.ppermute(sent, "tm", [(i, i ^ 2) for i in range(steps)])
+        parts = pl.pallas_call(
+            spread_kernel,
+            out_shape=(jax.ShapeDtypeStruct((8, LANES), jnp.float32),) * 4,
+            in_specs=vmem(2),
+            out_specs=tuple(vmem(4)),
+            compiler_params=limit,
+            cost_estimate=small,
+            name="spread_latents",
+        )(kept, other)
+        parts = [parts[0]] + [
+            lax.ppermute(parts[flip], plane_axes, [(i, i ^ flip) for i in range(plane)])
+            for flip in (1, 2, 3)
+        ]
+        here = pl.pallas_call(
+            clips_kernel,
+            out_shape=jax.ShapeDtypeStruct((2, TILE, LANES), jnp.float32),
+            in_specs=vmem(4),
+            out_specs=vmem(1)[0],
+            scratch_shapes=[pltpu.VMEM((4, 8, LANES), jnp.float32)],
+            compiler_params=limit,
+            cost_estimate=small,
+            name="clip_latents",
+        )(*parts)
+        sums = [here] + [
+            lax.ppermute(here, "dp", [(i, (i + step) % clips) for i in range(clips)])
+            for step in range(1, clips)
+        ]
 
     heads = qkv_weight.shape[1] // (3 * HD)
     frames = clip_inputs.shape[1]
@@ -729,14 +774,14 @@
     latents, query, key, value = pl.pallas_call(
         token_kernel,
         out_shape=(jax.ShapeDtypeStruct((1, 2, 2, 256), jnp.float32), tokens, tokens, tokens),
-        in_specs=vmem(6),
+        in_specs=vmem(9),
         out_specs=tuple(vmem(4)),
         scratch_shapes=[pltpu.VMEM((plane, 8, 6 * HD), jnp.float32)],
         compiler_params=limit,
         cost_estimate=pl.CostEstimate(flops=10**8, bytes_accessed=10**6, transcendentals=0),
         name="tokens",
     )(
-        partials,
+        *sums,
         *shares,
         table,
     )

time: 48.8 us -> 55.1 us (1.13)
  starting transfers between devices: 23.8 us -> 27.1 us
  waiting for transfers between devices: 11.8 us -> 14.7 us
  local copies, waits for them, and re-layouts: 0.7 us -> 1.44 us
  Pallas kernels: 10.6 us -> 10 us
    ppermute x0 -> x7, waiting for transfers between devices: none -> 7.95 us  [the longest x3 5.41 us: grouped(): lax.ppermute(parts[flip], plane_axes, [(i, i ^ flip) for i in range(plane)])]
    ppermute x0 -> x7, starting transfers between devices: none -> 6.8 us  [the longest x3 5 us: grouped(): lax.ppermute(here, 'dp', [(i, (i + step) % clips) for i in range(clips)])]
    all_to_all x1 -> x0, starting transfers between devices: 4.08 us -> none  [grouped(): partials = lax.all_to_all(partial, ('dp',) + plane_axes, 0, 0, tiled=True)]
    ppermute x3, waiting for transfers between devices: 3.67 us -> 0.01 us  [grouped(): shares.append(lax.ppermute(share, plane_axes, pairs))]
    ppermute x3, waiting for transfers between devices: 1.92 us -> 4.77 us  [grouped(): pieces.append(lax.ppermute(send if flip % 2 else keep, plane_axes, pairs))]
    ppermute x4, waiting for transfers between devices: 4.85 us -> 2 us  [grouped(): layers.append(lax.ppermute(own, ('dp', 'tm'), pairs))]
    all_to_all x1 -> x0, waiting for transfers between devices: 1.36 us -> none  [grouped(): partials = lax.all_to_all(partial, ('dp',) + plane_axes, 0, 0, tiled=True)]
    unnamed x10, local copies, waits for them, and re-layouts: 0.59 us -> 1.34 us
  transfers between devices with their start and end apart: 13 -> 19, of which waited for: 8 -> 9; matrix products, arithmetic and copies ran while one was open for 0% -> 0% of each run, Pallas kernels for 8% -> 10%
where the time goes in v1:
time: 55.1 us; the launch traced here: 54.7 us
  starting transfers between devices  27.1 us (49%)
  waiting for transfers between devices  14.7 us (27%)
  Pallas kernels  10 us (18%)
  local copies, waits for them, and re-layouts  1.44 us (3%)
  between operations  1.44 us (3%)
    ppermute x4, starting transfers between devices, grouped(): layers.append(lax.ppermute(own, ('dp', 'tm'), pairs))  7.17 us
    ppermute x3, waiting for transfers between devices, grouped(): lax.ppermute(parts[flip], plane_axes, [(i, i ^ flip) for i in range(plane)])  5.41 us
    all_to_all x1, starting transfers between devices, grouped(): weight = lax.all_to_all(packed, plane_axes, 0, 0, tiled=True)  5.31 us
    ppermute x3, starting transfers between devices, grouped(): lax.ppermute(here, 'dp', [(i, (i + step) % clips) for i in range(clips)])  5 us
    ppermute x3, waiting for transfers between devices, grouped(): pieces.append(lax.ppermute(send if flip % 2 else keep, plane_axes, pairs))  4.77 us
    ppermute x3, starting transfers between devices, grouped(): shares.append(lax.ppermute(share, plane_axes, pairs))  4.09 us
    ppermute x3, starting transfers between devices, grouped(): pieces.append(lax.ppermute(send if flip % 2 else keep, plane_axes, pairs))  3.61 us
    pallas_call x1, Pallas kernels, grouped(): pl.pallas_call(pack_kernel, out_shape=(jax.ShapeDtypeStruct((plane, 2 * G...  2.87 us
  transfers between devices with their start and end apart: 19, of which 9 were waited for; matrix products, arithmetic and copies ran while one was open for 0% of the time, Pallas kernels for 10%

profile of v1, /device:TPU:0, one launch (start us, length us, event | category | flops | bytes accessed | tf_op | source)
XLA Modules:
  0.0 54.7 jit_solution(14104567029486892468)
XLA Ops:
  0.6 2.9 %pack_weights.1 = (bf16[8,32,1920]{2,1,0:T(8,128)(2,1)}, f32[8,128]{1,0:T(8,128)}) custom-call(bf16[1728,128]{1,0:T(8,128)(2,1)} %w_hbm.1, bf16[384,768]{1,0:T(8,128)(2,1)} %qkv_hbm.3, bf16[64,3072]{1,0:T(8,128)(2,1)} %patch_hbm.1, bf16[3072]{0:T(1024)(128)(2,1)} %patch_bias_hbm.1), custom_call_target="tpu_custom_call" | custom-call | flops 100000000 | bytes 1000000 | tf_op jit(solution)/shard_map/weight_by_group/pack_weights/pallas_call | solution.py:623
  3.5 5.3 %all-to-all-start = ((bf16[8,32,1920]{2,1,0:T(8,128)(2,1)}), bf16[8,32,1920]{2,1,0:T(8,128)(2,1)S(1)}, u32[]{:S(2)}, u32[]{:S(2)}) async-start(bf16[8,32,1920]{2,1,0:T(8,128)(2,1)} %get-tuple-element.26), calls=%async_computation | async-start | bytes 1966080 | tf_op jit(solution)/shard_map/weight_by_group/all_to_all | solution.py:644
  8.9 0.7 %collective-permute-start = (bf16[64,512]{1,0:T(8,128)(2,1)S(1)}, bf16[64,512]{1,0:T(8,128)(2,1)S(1)}, u32[]{:S(2)}, u32[]{:S(2)}) collective-permute-start(bf16[64,512]{1,0:T(8,128)(2,1)S(1)} %bitcast.18), channel_id=1, source_target_pairs={{0,0},{2,8},{4,4},{6,12},{8,2},{10,10},{12,6},{14,14},{16,16},{18,... | collective-permute-start | bytes 196616 | tf_op jit(solution)/shard_map/gather_clips/ppermute | solution.py:671
  9.5 3.4 %collective-permute-start.1 = (bf16[64,512]{1,0:T(8,128)(2,1)S(1)}, bf16[64,512]{1,0:T(8,128)(2,1)S(1)}, u32[]{:S(2)}, u32[]{:S(2)}) collective-permute-start(bf16[64,512]{1,0:T(8,128)(2,1)S(1)} %bitcast.19), channel_id=1, source_target_pairs={{0,8},{2,16},{4,12},{6,20},{8,10},{10,18},{12,14},{14,22},{16,24},... | collective-permute-start | bytes 196616 | tf_op jit(solution)/shard_map/gather_clips/ppermute | solution.py:671
  13.0 2.6 %collective-permute-start.2 = (bf16[64,512]{1,0:T(8,128)(2,1)S(1)}, bf16[64,512]{1,0:T(8,128)(2,1)S(1)}, u32[]{:S(2)}, u32[]{:S(2)}) collective-permute-start(bf16[64,512]{1,0:T(8,128)(2,1)S(1)} %bitcast.20), channel_id=1, source_target_pairs={{0,16},{2,24},{4,20},{6,28},{8,18},{10,26},{12,22},{14,30},{16,0},... | collective-permute-start | bytes 196616 | tf_op jit(solution)/shard_map/gather_clips/ppermute | solution.py:671
  15.5 0.5 collective-permute-start.3
  16.7 2.2 %tables.1 = (f32[64,2]{1,0:T(8,128)}, f32[56,128]{1,0:T(8,128)}) custom-call(s32[2]{0:T(128)} %frame_ref.1, s32[1]{0:T(128)S(6)} %copy.22.row_pos_ref, f32[1,128]{1,0:T(1,128)} %constant.27.clone.freq_ref, bf16[128]{0:T(256)(128)(2,1)} %gain_hbm.1, bf16[128]{0:T(256)(128)(2,1)} %bias_hbm.1, f32[16]{0:T(128)} %out_bias_hbm.1, bf16[768]{0:T(1024)(128)(2,1)} %qkv_hbm.2, ...), custom_call_target="tpu_custom_call" | custom-call | flops 1000000 | bytes 1000000 | tf_op jit(solution)/shard_map/tables/tables/pallas_call | solution.py:648
  18.9 2.0 %collective-permute-done.2.refs_2_ = bf16[64,512]{1,0:T(8,128)(2,1)S(1)} collective-permute-done((bf16[64,512]{1,0:T(8,128)(2,1)S(1)}, bf16[64,512]{1,0:T(8,128)(2,1)S(1)}, u32[]{:S(2)}, u32[]{:S(2)}) %collective-permute-start.2) | collective-permute-done | bytes 65568 | tf_op jit(solution)/shard_map/gather_clips/ppermute | solution.py:671
  20.9 0.7 %copy-done.1 = f32[56,128]{1,0:T(8,128)S(1)} copy-done((f32[56,128]{1,0:T(8,128)S(1)}, f32[56,128]{1,0:T(8,128)}, u32[]{:S(2)}) %copy-start.1) | copy-done | bytes 28696
  21.7 2.1 %collective-permute-start.4 = (bf16[2,64,512]{2,1,0:T(8,128)(2,1)S(1)}, bf16[2,64,512]{2,1,0:T(8,128)(2,1)S(1)}, u32[]{:S(2)}, u32[]{:S(2)}) collective-permute-start(bf16[2,64,512]{2,1,0:T(8,128)(2,1)S(1)} %get-tuple-element.25), channel_id=1, source_target_pairs={{0,1},{1,0},{2,3},{3,2},{4,5},{5,4},{6,7},{7,6},{8,9},{9,8},{10,11... | collective-permute-start | bytes 393224 | tf_op jit(solution)/shard_map/spread_clips/ppermute | solution.py:687
  23.8 1.5 %collective-permute-start.5 = (bf16[2,64,512]{2,1,0:T(8,128)(2,1)S(1)}, bf16[2,64,512]{2,1,0:T(8,128)(2,1)S(1)}, u32[]{:S(2)}, u32[]{:S(2)}) collective-permute-start(bf16[2,64,512]{2,1,0:T(8,128)(2,1)S(1)} %get-tuple-element.24.x0_ref), channel_id=1, source_target_pairs={{0,4},{1,5},{2,6},{3,7},{4,0},{5,1},{6,2},{7,3},{8,12},{9,13},{10,... | collective-permute-start | bytes 393224 | tf_op jit(solution)/shard_map/spread_clips/ppermute | solution.py:687
  25.4 0.6 %copy-done.2 = f32[8,128]{1,0:T(8,128)S(1)} copy-done((f32[8,128]{1,0:T(8,128)S(1)}, f32[8,128]{1,0:T(8,128)}, u32[]{:S(2)}) %copy-start.2) | copy-done | bytes 4120
  26.0 0.2 join_weights.1.wt_ref
  26.3 1.5 %collective-permute-done.4.x1_ref = bf16[2,64,512]{2,1,0:T(8,128)(2,1)S(1)} collective-permute-done((bf16[2,64,512]{2,1,0:T(8,128)(2,1)S(1)}, bf16[2,64,512]{2,1,0:T(8,128)(2,1)S(1)}, u32[]{:S(2)}, u32[]{:S(2)}) %collective-permute-start.4) | collective-permute-done | bytes 131104 | tf_op jit(solution)/shard_map/spread_clips/ppermute | solution.py:687
  27.8 1.9 %collective-permute-done.5.x2_ref = bf16[2,64,512]{2,1,0:T(8,128)(2,1)S(1)} collective-permute-done((bf16[2,64,512]{2,1,0:T(8,128)(2,1)S(1)}, bf16[2,64,512]{2,1,0:T(8,128)(2,1)S(1)}, u32[]{:S(2)}, u32[]{:S(2)}) %collective-permute-start.5) | collective-permute-done | bytes 131104 | tf_op jit(solution)/shard_map/spread_clips/ppermute | solution.py:687
  29.7 1.4 %collective-permute-done.6.x3_ref = bf16[2,64,512]{2,1,0:T(8,128)(2,1)S(1)} collective-permute-done((bf16[2,64,512]{2,1,0:T(8,128)(2,1)S(1)}, bf16[2,64,512]{2,1,0:T(8,128)(2,1)S(1)}, u32[]{:S(2)}, u32[]{:S(2)}) %collective-permute-start.6) | collective-permute-done | bytes 131104 | tf_op jit(solution)/shard_map/spread_clips/ppermute | solution.py:687
  31.1 1.2 %own_channels.1 = (bf16[32,512]{1,0:T(8,128)(2,1)S(1)}, bf16[8,64,512]{2,1,0:T(8,128)(2,1)S(1)}) custom-call(bf16[2,64,512]{2,1,0:T(8,128)(2,1)S(1)} %get-tuple-element.24.x0_ref, bf16[2,64,512]{2,1,0:T(8,128)(2,1)S(1)} %collective-permute-done.4.x1_ref, bf16[2,64,512]{2,1,0:T(8,128)(2,1)S(1)} %collective-permute-done.5.x2_ref, ...), custom_call_target="tpu_custom_call" | custom-call | flops 40000000000 | bytes 1000000 | tf_op jit(solution)/shard_map/own_channels/pallas_call | solution.py:713
  32.4 0.6 %collective-permute-start.15 = (bf16[2,16,512]{2,1,0:T(8,128)(2,1)S(1)}, bf16[2,16,512]{2,1,0:T(8,128)(2,1)S(1)}, u32[]{:S(2)}, u32[]{:S(2)}) collective-permute-start(bf16[2,16,512]{2,1,0:T(8,128)(2,1)S(1)} %pad_maximum_fusion.m0_ref), channel_id=1, source_target_pairs={{0,1},{1,0},{2,3},{3,2},{4,5},{5,4},{6,7},{7,6},{8,9},{9,8},{10,11... | collective-permute-start | bytes 98312 | tf_op jit(solution)/shard_map/merged_projection/ppermute | solution.py:708
  33.0 1.7 %convolutions.1 = (f32[2,16,128]{2,1,0:T(8,128)S(1)}, f32[2,16,128]{2,1,0:T(8,128)S(1)}) custom-call(bf16[8,64,512]{2,1,0:T(8,128)(2,1)S(1)} %get-tuple-element.29.x_ref, bf16[32,512]{1,0:T(8,128)(2,1)S(1)} %get-tuple-element.30.normed_ref, bf16[880,512]{1,0:T(8,128)(2,1)S(1)} %collective-permute-done.7.wt_ref, f32[64,2]{1,0:T(8,128)S(1)} %copy-done.3, ...), custom_call_target="tpu_custom_call" | custom-call | flops 467140608 | bytes 1000000 | tf_op jit(solution)/shard_map/convolutions/pallas_call | solution.py:726
  34.7 0.6 %collective-permute-start.8 = (f32[2,16,128]{2,1,0:T(8,128)S(1)}, f32[2,16,128]{2,1,0:T(8,128)S(1)}, u32[]{:S(2)}, u32[]{:S(2)}) collective-permute-start(f32[2,16,128]{2,1,0:T(8,128)S(1)} %get-tuple-element.32), channel_id=1, source_target_pairs={{0,4},{2,6},{4,0},{6,2},{1,5},{3,7},{5,1},{7,3},{8,12},{10,14},{12... | collective-permute-start | bytes 49160 | tf_op jit(solution)/shard_map/sum_latents/ppermute | solution.py:742
  35.3 1.5 %collective-permute-start.16 = (bf16[2,16,512]{2,1,0:T(8,128)(2,1)S(1)}, bf16[2,16,512]{2,1,0:T(8,128)(2,1)S(1)}, u32[]{:S(2)}, u32[]{:S(2)}) collective-permute-start(bf16[2,16,512]{2,1,0:T(8,128)(2,1)S(1)} %pad_maximum_fusion.m0_ref), channel_id=1, source_target_pairs={{0,4},{1,5},{2,6},{3,7},{4,0},{5,1},{6,2},{7,3},{8,12},{9,13},{10,... | collective-permute-start | bytes 98312 | tf_op jit(solution)/shard_map/merged_projection/ppermute | solution.py:708
  36.8 1.9 %collective-permute-start.17 = (bf16[2,16,512]{2,1,0:T(8,128)(2,1)S(1)}, bf16[2,16,512]{2,1,0:T(8,128)(2,1)S(1)}, u32[]{:S(2)}, u32[]{:S(2)}) collective-permute-start(bf16[2,16,512]{2,1,0:T(8,128)(2,1)S(1)} %pad_maximum_fusion.m0_ref), channel_id=1, source_target_pairs={{0,5},{1,4},{2,7},{3,6},{4,1},{5,0},{6,3},{7,2},{8,13},{9,12},{10,... | collective-permute-start | bytes 98312 | tf_op jit(solution)/shard_map/merged_projection/ppermute | solution.py:708
  38.8 1.2 %collective-permute-start.9 = (f32[8,128]{1,0:T(8,128)S(1)}, f32[8,128]{1,0:T(8,128)S(1)}, u32[]{:S(2)}, u32[]{:S(2)}) collective-permute-start(f32[8,128]{1,0:T(8,128)S(1)} %get-tuple-element.34), channel_id=1, source_target_pairs={{0,1},{1,0},{2,3},{3,2},{4,5},{5,4},{6,7},{7,6},{8,9},{9,8},{10,11... | collective-permute-start | bytes 12296 | tf_op jit(solution)/shard_map/sum_latents/ppermute | solution.py:753
  40.1 2.4 %collective-permute-done.9.p1_ref = f32[8,128]{1,0:T(8,128)S(1)} collective-permute-done((f32[8,128]{1,0:T(8,128)S(1)}, f32[8,128]{1,0:T(8,128)S(1)}, u32[]{:S(2)}, u32[]{:S(2)}) %collective-permute-start.9) | collective-permute-done | bytes 4128 | tf_op jit(solution)/shard_map/sum_latents/ppermute | solution.py:753
  42.5 3.0 %collective-permute-done.11.p3_ref = f32[8,128]{1,0:T(8,128)S(1)} collective-permute-done((f32[8,128]{1,0:T(8,128)S(1)}, f32[8,128]{1,0:T(8,128)S(1)}, u32[]{:S(2)}, u32[]{:S(2)}) %collective-permute-start.11) | collective-permute-done | bytes 4128 | tf_op jit(solution)/shard_map/sum_latents/ppermute | solution.py:753
  45.6 1.5 %collective-permute-start.12 = (f32[2,16,128]{2,1,0:T(8,128)S(1)}, f32[2,16,128]{2,1,0:T(8,128)S(1)}, u32[]{:S(2)}, u32[]{:S(2)}) collective-permute-start(f32[2,16,128]{2,1,0:T(8,128)S(1)} %clip_latents.1.p0_ref), channel_id=1, source_target_pairs={{0,8},{8,16},{16,24},{24,0},{1,9},{9,17},{17,25},{25,1},{2,10},{10... | collective-permute-start | bytes 49160 | tf_op jit(solution)/shard_map/sum_latents/ppermute | solution.py:767
  47.1 2.3 %collective-permute-start.13 = (f32[2,16,128]{2,1,0:T(8,128)S(1)}, f32[2,16,128]{2,1,0:T(8,128)S(1)}, u32[]{:S(2)}, u32[]{:S(2)}) collective-permute-start(f32[2,16,128]{2,1,0:T(8,128)S(1)} %clip_latents.1.p0_ref), channel_id=1, source_target_pairs={{0,16},{8,24},{16,0},{24,8},{1,17},{9,25},{17,1},{25,9},{2,18},{10... | collective-permute-start | bytes 49160 | tf_op jit(solution)/shard_map/sum_latents/ppermute | solution.py:767
  49.4 1.2 %collective-permute-start.14 = (f32[2,16,128]{2,1,0:T(8,128)S(1)}, f32[2,16,128]{2,1,0:T(8,128)S(1)}, u32[]{:S(2)}, u32[]{:S(2)}) collective-permute-start(f32[2,16,128]{2,1,0:T(8,128)S(1)} %clip_latents.1.p0_ref), channel_id=1, source_target_pairs={{0,24},{8,0},{16,8},{24,16},{1,25},{9,1},{17,9},{25,17},{2,26},{10... | collective-permute-start | bytes 49160 | tf_op jit(solution)/shard_map/sum_latents/ppermute | solution.py:767
  50.6 0.5 collective-permute-done.12.p1_ref
  51.1 0.6 %collective-permute-done.13.p2_ref = f32[2,16,128]{2,1,0:T(8,128)S(1)} collective-permute-done((f32[2,16,128]{2,1,0:T(8,128)S(1)}, f32[2,16,128]{2,1,0:T(8,128)S(1)}, u32[]{:S(2)}, u32[]{:S(2)}) %collective-permute-start.13) | collective-permute-done | bytes 16416 | tf_op jit(solution)/shard_map/sum_latents/ppermute | solution.py:767
  51.7 1.4 %collective-permute-done.14.p3_ref = f32[2,16,128]{2,1,0:T(8,128)S(1)} collective-permute-done((f32[2,16,128]{2,1,0:T(8,128)S(1)}, f32[2,16,128]{2,1,0:T(8,128)S(1)}, u32[]{:S(2)}, u32[]{:S(2)}) %collective-permute-start.14) | collective-permute-done | bytes 16416 | tf_op jit(solution)/shard_map/sum_latents/ppermute | solution.py:767
  53.1 1.6 %tokens.1 = (f32[1,2,2,256]{3,2,1,0:T(2,128)}, bf16[8,8,256]{2,1,0:T(8,128)(2,1)}, bf16[8,8,256]{2,1,0:T(8,128)(2,1)}, bf16[8,8,256]{2,1,0:T(8,128)(2,1)}) custom-call(f32[2,16,128]{2,1,0:T(8,128)S(1)} %clip_latents.1.p0_ref, f32[2,16,128]{2,1,0:T(8,128)S(1)} %collective-permute-done.12.p1_ref, f32[2,16,128]{2,1,0:T(8,128)S(1)} %collective-permute-done.13.p2_ref, ...), custom_call_target="tpu_custom_call" | custom-call | flops 100000000 | bytes 1000000 | tf_op jit(solution)/shard_map/tokens/pallas_call | solution.py:774
  (29 shorter events, 0.5 us)
Async XLA Ops:
  0.6 24.7 %copy-start = (bf16[27,128,16]{1,2,0:T(8,128)(2,1)S(1)}, bf16[27,128,16]{1,2,0:T(8,128)(2,1)}, u32[]{:S(2)}) copy-start(bf16[27,128,16]{1,2,0:T(8,128)(2,1)} %param.19) | copy-start | bytes 331780
  3.5 5.3 %copy-start.4 = (bf16[1,2,2,16,512]{4,3,2,1,0:T(8,128)(2,1)S(1)}, bf16[1,2,2,16,512]{4,3,2,1,0:T(8,128)(2,1)}, u32[]{:S(2)}) copy-start(bf16[1,2,2,16,512]{4,3,2,1,0:T(8,128)(2,1)} %param.15) | copy-start | bytes 196612
  3.5 21.9 %all-to-all-start = ((bf16[8,32,1920]{2,1,0:T(8,128)(2,1)}), bf16[8,32,1920]{2,1,0:T(8,128)(2,1)S(1)}, u32[]{:S(2)}, u32[]{:S(2)}) async-start(bf16[8,32,1920]{2,1,0:T(8,128)(2,1)} %get-tuple-element.26), calls=%async_computation | async-start | bytes 1966080 | tf_op jit(solution)/shard_map/weight_by_group/all_to_all | solution.py:644
  8.9 10.0 %collective-permute-start = (bf16[64,512]{1,0:T(8,128)(2,1)S(1)}, bf16[64,512]{1,0:T(8,128)(2,1)S(1)}, u32[]{:S(2)}, u32[]{:S(2)}) collective-permute-start(bf16[64,512]{1,0:T(8,128)(2,1)S(1)} %bitcast.18), channel_id=1, source_target_pairs={{0,0},{2,8},{4,4},{6,12},{8,2},{10,10},{12,6},{14,14},{16,16},{18,... | collective-permute-start | bytes 196616 | tf_op jit(solution)/shard_map/gather_clips/ppermute | solution.py:671
  9.5 9.4 %collective-permute-start.1 = (bf16[64,512]{1,0:T(8,128)(2,1)S(1)}, bf16[64,512]{1,0:T(8,128)(2,1)S(1)}, u32[]{:S(2)}, u32[]{:S(2)}) collective-permute-start(bf16[64,512]{1,0:T(8,128)(2,1)S(1)} %bitcast.19), channel_id=1, source_target_pairs={{0,8},{2,16},{4,12},{6,20},{8,10},{10,18},{12,14},{14,22},{16,24},... | collective-permute-start | bytes 196616 | tf_op jit(solution)/shard_map/gather_clips/ppermute | solution.py:671
  13.0 7.9 %collective-permute-start.2 = (bf16[64,512]{1,0:T(8,128)(2,1)S(1)}, bf16[64,512]{1,0:T(8,128)(2,1)S(1)}, u32[]{:S(2)}, u32[]{:S(2)}) collective-permute-start(bf16[64,512]{1,0:T(8,128)(2,1)S(1)} %bitcast.20), channel_id=1, source_target_pairs={{0,16},{2,24},{4,20},{6,28},{8,18},{10,26},{12,22},{14,30},{16,0},... | collective-permute-start | bytes 196616 | tf_op jit(solution)/shard_map/gather_clips/ppermute | solution.py:671
  15.5 5.3 %collective-permute-start.3 = (bf16[64,512]{1,0:T(8,128)(2,1)S(1)}, bf16[64,512]{1,0:T(8,128)(2,1)S(1)}, u32[]{:S(2)}, u32[]{:S(2)}) collective-permute-start(bf16[64,512]{1,0:T(8,128)(2,1)S(1)} %bitcast.21), channel_id=1, source_target_pairs={{0,24},{2,0},{4,28},{6,4},{8,26},{10,2},{12,30},{14,6},{16,8},{18,... | collective-permute-start | bytes 196616 | tf_op jit(solution)/shard_map/gather_clips/ppermute | solution.py:671
  20.9 0.7 %copy-start.1 = (f32[56,128]{1,0:T(8,128)S(1)}, f32[56,128]{1,0:T(8,128)}, u32[]{:S(2)}) copy-start(f32[56,128]{1,0:T(8,128)} %get-tuple-element.23.refs_4_) | copy-start | bytes 86020
  21.7 6.1 %collective-permute-start.4 = (bf16[2,64,512]{2,1,0:T(8,128)(2,1)S(1)}, bf16[2,64,512]{2,1,0:T(8,128)(2,1)S(1)}, u32[]{:S(2)}, u32[]{:S(2)}) collective-permute-start(bf16[2,64,512]{2,1,0:T(8,128)(2,1)S(1)} %get-tuple-element.25), channel_id=1, source_target_pairs={{0,1},{1,0},{2,3},{3,2},{4,5},{5,4},{6,7},{7,6},{8,9},{9,8},{10,11... | collective-permute-start | bytes 393224 | tf_op jit(solution)/shard_map/spread_clips/ppermute | solution.py:687
  23.8 5.9 %collective-permute-start.5 = (bf16[2,64,512]{2,1,0:T(8,128)(2,1)S(1)}, bf16[2,64,512]{2,1,0:T(8,128)(2,1)S(1)}, u32[]{:S(2)}, u32[]{:S(2)}) collective-permute-start(bf16[2,64,512]{2,1,0:T(8,128)(2,1)S(1)} %get-tuple-element.24.x0_ref), channel_id=1, source_target_pairs={{0,4},{1,5},{2,6},{3,7},{4,0},{5,1},{6,2},{7,3},{8,12},{9,13},{10,... | collective-permute-start | bytes 393224 | tf_op jit(solution)/shard_map/spread_clips/ppermute | solution.py:687
  25.2 5.9 %collective-permute-start.6 = (bf16[2,64,512]{2,1,0:T(8,128)(2,1)S(1)}, bf16[2,64,512]{2,1,0:T(8,128)(2,1)S(1)}, u32[]{:S(2)}, u32[]{:S(2)}) collective-permute-start(bf16[2,64,512]{2,1,0:T(8,128)(2,1)S(1)} %get-tuple-element.25), channel_id=1, source_target_pairs={{0,5},{1,4},{2,7},{3,6},{4,1},{5,0},{6,3},{7,2},{8,13},{9,12},{10,... | collective-permute-start | bytes 393224 | tf_op jit(solution)/shard_map/spread_clips/ppermute | solution.py:687
  25.3 0.7 %copy-start.2 = (f32[8,128]{1,0:T(8,128)S(1)}, f32[8,128]{1,0:T(8,128)}, u32[]{:S(2)}) copy-start(f32[8,128]{1,0:T(8,128)} %get-tuple-element.27.lines_ref) | copy-start | bytes 12292
  26.0 5.1 %copy-start.3 = (f32[64,2]{1,0:T(8,128)S(1)}, f32[64,2]{1,0:T(8,128)}, u32[]{:S(2)}) copy-start(f32[64,2]{1,0:T(8,128)} %get-tuple-element.28.scale_ref) | copy-start | bytes 1540
  26.2 6.1 %collective-permute-start.7 = (bf16[880,512]{1,0:T(8,128)(2,1)S(1)}, bf16[880,512]{1,0:T(8,128)(2,1)S(1)}, u32[]{:S(2)}, u32[]{:S(2)}) collective-permute-start(bf16[880,512]{1,0:T(8,128)(2,1)S(1)} %join_weights.1.wt_ref), channel_id=1, source_target_pairs={{0,2},{2,0},{4,6},{6,4},{1,3},{3,1},{5,7},{7,5},{8,10},{10,8},{12,... | collective-permute-start | bytes 2703368 | tf_op jit(solution)/shard_map/join_weights/ppermute | solution.py:702
  32.4 17.0 %collective-permute-start.15 = (bf16[2,16,512]{2,1,0:T(8,128)(2,1)S(1)}, bf16[2,16,512]{2,1,0:T(8,128)(2,1)S(1)}, u32[]{:S(2)}, u32[]{:S(2)}) collective-permute-start(bf16[2,16,512]{2,1,0:T(8,128)(2,1)S(1)} %pad_maximum_fusion.m0_ref), channel_id=1, source_target_pairs={{0,1},{1,0},{2,3},{3,2},{4,5},{5,4},{6,7},{7,6},{8,9},{9,8},{10,11... | collective-permute-start | bytes 98312 | tf_op jit(solution)/shard_map/merged_projection/ppermute | solution.py:708
  34.7 4.0 %collective-permute-start.8 = (f32[2,16,128]{2,1,0:T(8,128)S(1)}, f32[2,16,128]{2,1,0:T(8,128)S(1)}, u32[]{:S(2)}, u32[]{:S(2)}) collective-permute-start(f32[2,16,128]{2,1,0:T(8,128)S(1)} %get-tuple-element.32), channel_id=1, source_target_pairs={{0,4},{2,6},{4,0},{6,2},{1,5},{3,7},{5,1},{7,3},{8,12},{10,14},{12... | collective-permute-start | bytes 49160 | tf_op jit(solution)/shard_map/sum_latents/ppermute | solution.py:742
  35.3 15.3 %collective-permute-start.16 = (bf16[2,16,512]{2,1,0:T(8,128)(2,1)S(1)}, bf16[2,16,512]{2,1,0:T(8,128)(2,1)S(1)}, u32[]{:S(2)}, u32[]{:S(2)}) collective-permute-start(bf16[2,16,512]{2,1,0:T(8,128)(2,1)S(1)} %pad_maximum_fusion.m0_ref), channel_id=1, source_target_pairs={{0,4},{1,5},{2,6},{3,7},{4,0},{5,1},{6,2},{7,3},{8,12},{9,13},{10,... | collective-permute-start | bytes 98312 | tf_op jit(solution)/shard_map/merged_projection/ppermute | solution.py:708
  36.8 13.8 %collective-permute-start.17 = (bf16[2,16,512]{2,1,0:T(8,128)(2,1)S(1)}, bf16[2,16,512]{2,1,0:T(8,128)(2,1)S(1)}, u32[]{:S(2)}, u32[]{:S(2)}) collective-permute-start(bf16[2,16,512]{2,1,0:T(8,128)(2,1)S(1)} %pad_maximum_fusion.m0_ref), channel_id=1, source_target_pairs={{0,5},{1,4},{2,7},{3,6},{4,1},{5,0},{6,3},{7,2},{8,13},{9,12},{10,... | collective-permute-start | bytes 98312 | tf_op jit(solution)/shard_map/merged_projection/ppermute | solution.py:708
  38.8 3.6 %collective-permute-start.9 = (f32[8,128]{1,0:T(8,128)S(1)}, f32[8,128]{1,0:T(8,128)S(1)}, u32[]{:S(2)}, u32[]{:S(2)}) collective-permute-start(f32[8,128]{1,0:T(8,128)S(1)} %get-tuple-element.34), channel_id=1, source_target_pairs={{0,1},{1,0},{2,3},{3,2},{4,5},{5,4},{6,7},{7,6},{8,9},{9,8},{10,11... | collective-permute-start | bytes 12296 | tf_op jit(solution)/shard_map/sum_latents/ppermute | solution.py:753
  40.1 2.4 %collective-permute-start.10 = (f32[8,128]{1,0:T(8,128)S(1)}, f32[8,128]{1,0:T(8,128)S(1)}, u32[]{:S(2)}, u32[]{:S(2)}) collective-permute-start(f32[8,128]{1,0:T(8,128)S(1)} %get-tuple-element.35), channel_id=1, source_target_pairs={{0,2},{1,3},{2,0},{3,1},{4,6},{5,7},{6,4},{7,5},{8,10},{9,11},{10,... | collective-permute-start | bytes 12296 | tf_op jit(solution)/shard_map/sum_latents/ppermute | solution.py:753
  42.4 3.0 %collective-permute-start.11 = (f32[8,128]{1,0:T(8,128)S(1)}, f32[8,128]{1,0:T(8,128)S(1)}, u32[]{:S(2)}, u32[]{:S(2)}) collective-permute-start(f32[8,128]{1,0:T(8,128)S(1)} %get-tuple-element.36), channel_id=1, source_target_pairs={{0,3},{1,2},{2,1},{3,0},{4,7},{5,6},{6,5},{7,4},{8,11},{9,10},{10,... | collective-permute-start | bytes 12296 | tf_op jit(solution)/shard_map/sum_latents/ppermute | solution.py:753
  45.6 5.5 %collective-permute-start.12 = (f32[2,16,128]{2,1,0:T(8,128)S(1)}, f32[2,16,128]{2,1,0:T(8,128)S(1)}, u32[]{:S(2)}, u32[]{:S(2)}) collective-permute-start(f32[2,16,128]{2,1,0:T(8,128)S(1)} %clip_latents.1.p0_ref), channel_id=1, source_target_pairs={{0,8},{8,16},{16,24},{24,0},{1,9},{9,17},{17,25},{25,1},{2,10},{10... | collective-permute-start | bytes 49160 | tf_op jit(solution)/shard_map/sum_latents/ppermute | solution.py:767
  47.1 4.6 %collective-permute-start.13 = (f32[2,16,128]{2,1,0:T(8,128)S(1)}, f32[2,16,128]{2,1,0:T(8,128)S(1)}, u32[]{:S(2)}, u32[]{:S(2)}) collective-permute-start(f32[2,16,128]{2,1,0:T(8,128)S(1)} %clip_latents.1.p0_ref), channel_id=1, source_target_pairs={{0,16},{8,24},{16,0},{24,8},{1,17},{9,25},{17,1},{25,9},{2,18},{10... | collective-permute-start | bytes 49160 | tf_op jit(solution)/shard_map/sum_latents/ppermute | solution.py:767
  49.4 3.7 %collective-permute-start.14 = (f32[2,16,128]{2,1,0:T(8,128)S(1)}, f32[2,16,128]{2,1,0:T(8,128)S(1)}, u32[]{:S(2)}, u32[]{:S(2)}) collective-permute-start(f32[2,16,128]{2,1,0:T(8,128)S(1)} %clip_latents.1.p0_ref), channel_id=1, source_target_pairs={{0,24},{8,0},{16,8},{24,16},{1,25},{9,1},{17,9},{25,17},{2,26},{10... | collective-permute-start | bytes 49160 | tf_op jit(solution)/shard_map/sum_latents/ppermute | solution.py:767
